TPU v7x, 32 devices: a whole 2x2x4 slice. The times are simulated.
32 devices in a mesh: wake: 16 (over z, y, core), col: 2 (over x).
Axes of the slice: x: 2, y: 2, z: 4, core: 2. Of those that a mesh axis runs over, the one named last changes fastest.
Arguments:
- points: float32 [3, 32768], P(None, ('wake', 'col')), may hold values from -6 to 6
- normals: float32 [3, 32768], P(None, ('wake', 'col')), may hold values from -6 to 6
- freestream: float32 [3], replicated, may hold values from -2 to 2
- wake_nodes: float32 [3, 16384], P(None, 'wake'), may hold values from -6 to 6
- circulation: float32 [16384], P('wake'), may hold values from -4 to 4
- filament: int32 [16384], P('wake'), may hold values from 0 to 127, never falling along the last dimension, each value on 1 to 256 neighbouring positions
- self_term: float32 [32768], P(('wake', 'col')), may hold values from 1 to 8
- near_blocks: float32 [256, 2, 1, 128, 128], P('wake', 'col'), may hold values from -0.5 to 0.5
- near_index: int32 [256, 2, 1], P('wake', 'col'), may hold values from 0 to 127
- far_left: float32 [2, 32, 32768], P('col', None, 'wake'), may hold values from -1 to 1
- far_right: float32 [16, 32, 32768], P('wake', None, 'col'), may hold values from -0.046875 to 0.046875
Outputs:
- right_side: float32 [32768], P(('wake', 'col'))
- strengths: float32 [32768], P(('wake', 'col'))
Inputs may be any that keep to these rules, and one draw needn't show every extreme that they name: Filament numbers never fall along the nodes; each filament has 1 to 256 nodes and one has exactly 256.
All inputs are finite; a program needn't handle non-finite values.
Results may differ from a plain program's by a relative error of at most 0.0004.
Values sent between devices are 32-bit elements; how exact they have to be, the bound alone decides.
No kernel may reach another device: no remote copies, remote signals or barrier semaphores. Data moves between devices by JAX's collectives and lax.ppermute only.
A program may use at most 64 MiB of HBM per device.

v0:
```python
import math

import jax
import jax.numpy as jnp
from jax import lax
from jax.sharding import PartitionSpec as P

KRYLOV = 6


core_sq = 0.01
four_pi = 4.0 * math.pi


def shifted(value, axis, steps):
    count = lax.axis_size(axis)
    first, last = (max(0, -steps), min(count, count - steps))
    return lax.ppermute(value, axis, [(source, source + steps) for source in range(first, last)])


def induce(points, normals, segments):
    near_arm = points[:, :, None] - segments[0:3, None, :]
    far_arm = points[:, :, None] - segments[3:6, None, :]
    cross_x = near_arm[1] * far_arm[2] - near_arm[2] * far_arm[1]
    cross_y = near_arm[2] * far_arm[0] - near_arm[0] * far_arm[2]
    cross_z = near_arm[0] * far_arm[1] - near_arm[1] * far_arm[0]
    normal_part = (
        cross_x * normals[0][:, None]
        + cross_y * normals[1][:, None]
        + cross_z * normals[2][:, None]
    )
    near_len = jnp.sqrt(jnp.sum(near_arm * near_arm, axis=0))
    far_len = jnp.sqrt(jnp.sum(far_arm * far_arm, axis=0))
    inner_dot = jnp.sum(near_arm * far_arm, axis=0)
    factor = (
        segments[6][None, :]
        * (near_len + far_len)
        / (four_pi * (near_len * far_len * (near_len * far_len + inner_dot) + core_sq))
    )
    return jnp.sum(factor * normal_part, axis=1)


def small_solve(gram_matrix, projected):
    size_now = gram_matrix.shape[0]
    factor = [[None for inner_pos in range(size_now)] for outer_pos in range(size_now)]
    for outer_pos in range(size_now):
        for inner_pos in range(outer_pos + 1):
            partial_sum = gram_matrix[outer_pos, inner_pos]
            for middle in range(inner_pos):
                partial_sum = partial_sum - factor[outer_pos][middle] * factor[inner_pos][middle]
            if inner_pos == outer_pos:
                factor[outer_pos][inner_pos] = jnp.sqrt(partial_sum)
            else:
                factor[outer_pos][inner_pos] = partial_sum / factor[inner_pos][inner_pos]
    forward = []
    for outer_pos in range(size_now):
        partial_sum = projected[outer_pos]
        for middle in range(outer_pos):
            partial_sum = partial_sum - factor[outer_pos][middle] * forward[middle]
        forward.append(partial_sum / factor[outer_pos][outer_pos])
    backward = [None for outer_pos in range(size_now)]
    for outer_pos in reversed(range(size_now)):
        partial_sum = forward[outer_pos]
        for middle in range(outer_pos + 1, size_now):
            partial_sum = partial_sum - factor[middle][outer_pos] * backward[middle]
        backward[outer_pos] = partial_sum / factor[outer_pos][outer_pos]
    return backward


def body(
    points,
    normals,
    freestream,
    wake_nodes,
    circulation,
    filament,
    self_term,
    near_blocks,
    near_index,
    far_left,
    far_right,
):
    highest = lax.Precision.HIGHEST
    piece_len = points.shape[1]
    filament_tag = filament.astype(jnp.float32) + 1.0
    first_node = jnp.concatenate([wake_nodes[:, 0], filament_tag[0:1]])
    following = shifted(first_node, "wake", -1)
    end_points = jnp.concatenate([wake_nodes[:, 1:], following[0:3, None]], axis=1)
    next_tag = jnp.concatenate([filament_tag[1:], following[3:4]])
    link_mask = (filament_tag == next_tag).astype(jnp.float32)
    segments = jnp.concatenate([wake_nodes, end_points, (circulation * link_mask)[None, :]], axis=0)
    shard_segs = lax.all_gather(segments, "wake", axis=1, tiled=True)
    seg_count = shard_segs.shape[1]
    add_block_len = math.gcd(seg_count, 512)

    def add_block(position, running):
        segment_block = lax.dynamic_slice_in_dim(
            shard_segs, position * add_block_len, add_block_len, 1
        )
        return running + induce(points, normals, segment_block)

    induced = lax.fori_loop(
        0, seg_count // add_block_len, add_block, jnp.zeros((piece_len,), jnp.float32)
    )
    right_side = -(jnp.dot(freestream, normals, precision=highest) + induced)
    block_len = near_blocks.shape[-1]
    local_blocks = near_blocks[:, 0]
    local_index = near_index[:, 0]
    left_factor = far_left[0]
    right_factor = far_right[0]
    initial_sq = lax.psum(jnp.sum(right_side * right_side), ("wake", "col"))
    initial_norm = jnp.sqrt(initial_sq)
    krylov = [right_side / initial_norm]
    hessenberg = jnp.zeros((KRYLOV + 1, KRYLOV), jnp.float32)
    for column in range(KRYLOV):
        vector = krylov[column]
        column_vec = lax.all_gather(vector, "wake", axis=0, tiled=True)
        far_coeff = jnp.dot(right_factor, column_vec, precision=highest)
        column_blocks = column_vec.reshape(-1, block_len)
        selected = column_blocks[local_index]
        near_part = jnp.einsum("rkij,rkj->ri", local_blocks, selected, precision=highest).reshape(
            piece_len * lax.axis_size("col")
        )
        summed = lax.psum_scatter(
            near_part + jnp.dot(far_coeff, left_factor, precision=highest),
            "col",
            scatter_dimension=0,
            tiled=True,
        )
        image_vec = self_term * vector + summed
        local_dots = jnp.stack([jnp.sum(image_vec * member) for member in krylov])
        coeffs = lax.psum(local_dots, ("wake", "col"))
        remainder = image_vec
        for position in range(column + 1):
            remainder = remainder - coeffs[position] * krylov[position]
        new_norm = jnp.sqrt(lax.psum(jnp.sum(remainder * remainder), ("wake", "col")))
        hessenberg = (
            hessenberg.at[: column + 1, column].set(coeffs).at[column + 1, column].set(new_norm)
        )
        if column + 1 < KRYLOV:
            krylov.append(remainder / new_norm)
    gram_matrix = jnp.dot(hessenberg.T, hessenberg, precision=highest)
    combination = small_solve(gram_matrix, initial_norm * hessenberg[0])
    strengths = combination[0] * krylov[0]
    for position in range(1, KRYLOV):
        strengths = strengths + combination[position] * krylov[position]
    return (right_side, strengths)


def solution(mesh):
    in_specs = (
        P(None, ("wake", "col")),
        P(None, ("wake", "col")),
        P(),
        P(None, "wake"),
        P("wake"),
        P("wake"),
        P(("wake", "col")),
        P("wake", "col", None, None, None),
        P("wake", "col", None),
        P("col", None, "wake"),
        P("wake", None, "col"),
    )
    out_specs = (P(("wake", "col")), P(("wake", "col")))
    return jax.shard_map(body, mesh=mesh, in_specs=in_specs, out_specs=out_specs, check_vma=False)
```

profile of v0, /device:TPU:0, one launch (start us, length us, event | category | flops | bytes accessed | tf_op | source)
XLA Modules:
  0.0 1426.7 jit_solution(15136460085953510115)
XLA Ops:
  18.1 26.6 %all_gather.21 = f32[7,16384]{1,0:T(8,128)} all-gather(f32[7,1024]{1,0:T(8,128)S(1)} %pad_maximum_fusion), channel_id=1, replica_groups=mesh['wake'=16,'col'=2] {'wake'}, dimensions={1}, use_global_device_ids=true | all-gather | bytes 487424 | tf_op jit(solution)/shard_map/all_gather | solution.py:92
  44.7 603.5 %while.26 = (s32[]{:T(128)}, f32[1024]{0:T(1024)S(1)}, f32[7,16384]{1,0:T(8,128)}, f32[3,1024]{1,0:T(4,128)}, f32[3,1024]{1,0:T(4,128)}, /*index=5*/s32[]{:T(128...) while((s32[]{:T(128)}, f32[1024]{0:T(1024)S(1)}, f32[7,16384]{1,0:T(8,128)}, ...), condition=%wide.region_5.0_spmd.clone, body=%wide.region_0.0_spmd.clone.sunk | while | flops 23593992 | bytes 37906656 | solution.py:102
  45.6 9.2 multiply_reduce_fusion.32
  64.4 9.2 multiply_reduce_fusion.32
  83.3 9.2 multiply_reduce_fusion.32
  102.1 9.2 multiply_reduce_fusion.32
  121.0 9.2 multiply_reduce_fusion.32
  139.9 9.2 multiply_reduce_fusion.32
  158.7 9.2 multiply_reduce_fusion.32
  196.4 9.2 multiply_reduce_fusion.32
  215.3 9.2 multiply_reduce_fusion.32
  234.2 9.2 multiply_reduce_fusion.32
  253.0 9.2 multiply_reduce_fusion.32
  271.9 9.2 multiply_reduce_fusion.32
  290.7 9.2 multiply_reduce_fusion.32
  309.6 9.2 multiply_reduce_fusion.32
  347.3 9.2 multiply_reduce_fusion.32
  366.2 9.2 multiply_reduce_fusion.32
  385.0 9.2 multiply_reduce_fusion.32
  403.9 9.2 multiply_reduce_fusion.32
  422.7 9.2 multiply_reduce_fusion.32
  441.6 9.2 multiply_reduce_fusion.32
  460.5 9.2 multiply_reduce_fusion.32
  479.3 9.2 multiply_reduce_fusion.32
  498.2 9.2 multiply_reduce_fusion.32
  517.0 9.2 multiply_reduce_fusion.32
  554.8 9.2 multiply_reduce_fusion.32
  573.6 9.2 multiply_reduce_fusion.32
  592.5 9.2 multiply_reduce_fusion.32
  649.3 37.1 %psum.91 = f32[]{:T(128)} all-reduce(f32[]{:T(128)} %multiply_reduce_fusion.30), channel_id=1, replica_groups=mesh['wake'=16,'col'=2] {'wake','col'}, use_global_device_ids=true, to_apply=%region_7.0 | all-reduce | flops 1 | bytes 8 | tf_op jit(solution)/shard_map/psum | solution.py:111
  687.8 21.4 %all_gather.22 = f32[16384]{0:T(1024)S(1)} all-gather(f32[1024]{0:T(1024)S(1)} %get-tuple-element.307), channel_id=1, replica_groups=mesh['wake'=16,'col'=2] {'wake'}, dimensions={0}, use_global_device_ids=true | all-gather | bytes 69632 | tf_op jit(solution)/shard_map/all_gather | solution.py:117
  719.1 37.1 %psum.92 = f32[1]{0:T(128)} all-reduce(f32[1]{0:T(128)} %bitcast.18), channel_id=1, replica_groups=mesh['wake'=16,'col'=2] {'wake','col'}, use_global_device_ids=true, to_apply=%region_10.0 | all-reduce | flops 1 | bytes 8 | tf_op jit(solution)/shard_map/psum | solution.py:132
  757.5 42.8 %psum.93 = f32[]{:T(128)} all-reduce(f32[]{:T(128)} %get-tuple-element.305), channel_id=1, replica_groups=mesh['wake'=16,'col'=2] {'wake','col'}, use_global_device_ids=true, to_apply=%region_12.0 | all-reduce | flops 1 | bytes 8 | tf_op jit(solution)/shard_map/psum | solution.py:136
  800.9 20.9 %all_gather.23 = f32[16384]{0:T(1024)S(1)} all-gather(f32[1024]{0:T(1024)S(1)} %broadcast_divide_fusion.4), channel_id=1, replica_groups=mesh['wake'=16,'col'=2] {'wake'}, dimensions={0}, use_global_device_ids=true | all-gather | bytes 69632 | tf_op jit(solution)/shard_map/all_gather | solution.py:117
  833.8 36.8 %psum.94 = f32[2]{0:T(128)S(1)} all-reduce(f32[2]{0:T(128)S(1)} %pad_maximum_fusion.2), channel_id=1, replica_groups=mesh['wake'=16,'col'=2] {'wake','col'}, use_global_device_ids=true, to_apply=%region_17.0 | all-reduce | flops 2 | bytes 16 | tf_op jit(solution)/shard_map/psum | solution.py:132
  873.1 41.5 %psum.95 = f32[]{:T(128)} all-reduce(f32[]{:T(128)} %get-tuple-element.302), channel_id=1, replica_groups=mesh['wake'=16,'col'=2] {'wake','col'}, use_global_device_ids=true, to_apply=%region_19.0 | all-reduce | flops 1 | bytes 8 | tf_op jit(solution)/shard_map/psum | solution.py:136
  915.4 20.8 %all_gather.24 = f32[16384]{0:T(1024)S(1)} all-gather(f32[1024]{0:T(1024)S(1)} %broadcast_divide_fusion.3), channel_id=1, replica_groups=mesh['wake'=16,'col'=2] {'wake'}, dimensions={0}, use_global_device_ids=true | all-gather | bytes 69632 | tf_op jit(solution)/shard_map/all_gather | solution.py:117
  948.1 36.9 %psum.96 = f32[3]{0:T(128)S(1)} all-reduce(f32[3]{0:T(128)S(1)} %pad_maximum_fusion.3), channel_id=1, replica_groups=mesh['wake'=16,'col'=2] {'wake','col'}, use_global_device_ids=true, to_apply=%region_25.0 | all-reduce | flops 3 | bytes 24 | tf_op jit(solution)/shard_map/psum | solution.py:132
  988.1 42.5 %psum.97 = f32[]{:T(128)} all-reduce(f32[]{:T(128)} %get-tuple-element.299), channel_id=1, replica_groups=mesh['wake'=16,'col'=2] {'wake','col'}, use_global_device_ids=true, to_apply=%region_27.0 | all-reduce | flops 1 | bytes 8 | tf_op jit(solution)/shard_map/psum | solution.py:136
  1031.2 21.0 %all_gather.25 = f32[16384]{0:T(1024)S(1)} all-gather(f32[1024]{0:T(1024)S(1)} %broadcast_divide_fusion.2), channel_id=1, replica_groups=mesh['wake'=16,'col'=2] {'wake'}, dimensions={0}, use_global_device_ids=true | all-gather | bytes 69632 | tf_op jit(solution)/shard_map/all_gather | solution.py:117
  1065.4 36.8 %psum.98 = f32[4]{0:T(128)S(1)} all-reduce(f32[4]{0:T(128)S(1)} %pad_maximum_fusion.4), channel_id=1, replica_groups=mesh['wake'=16,'col'=2] {'wake','col'}, use_global_device_ids=true, to_apply=%region_34.0 | all-reduce | flops 4 | bytes 32 | tf_op jit(solution)/shard_map/psum | solution.py:132
  1105.9 41.6 %psum.99 = f32[]{:T(128)} all-reduce(f32[]{:T(128)} %get-tuple-element.296), channel_id=1, replica_groups=mesh['wake'=16,'col'=2] {'wake','col'}, use_global_device_ids=true, to_apply=%region_36.0 | all-reduce | flops 1 | bytes 8 | tf_op jit(solution)/shard_map/psum | solution.py:136
  1148.2 20.8 %all_gather.26 = f32[16384]{0:T(1024)S(1)} all-gather(f32[1024]{0:T(1024)S(1)} %broadcast_divide_fusion.1), channel_id=1, replica_groups=mesh['wake'=16,'col'=2] {'wake'}, dimensions={0}, use_global_device_ids=true | all-gather | bytes 69632 | tf_op jit(solution)/shard_map/all_gather | solution.py:117
  1182.2 36.8 %psum.100 = f32[5]{0:T(128)S(1)} all-reduce(f32[5]{0:T(128)S(1)} %stack.96), channel_id=1, replica_groups=mesh['wake'=16,'col'=2] {'wake','col'}, use_global_device_ids=true, to_apply=%region_44.0 | all-reduce | flops 5 | bytes 40 | tf_op jit(solution)/shard_map/psum | solution.py:132
  1223.4 42.4 %psum.101 = f32[]{:T(128)} all-reduce(f32[]{:T(128)} %get-tuple-element.293), channel_id=1, replica_groups=mesh['wake'=16,'col'=2] {'wake','col'}, use_global_device_ids=true, to_apply=%region_46.0 | all-reduce | flops 1 | bytes 8 | tf_op jit(solution)/shard_map/psum | solution.py:136
  1266.5 21.0 %all_gather.27 = f32[16384]{0:T(1024)S(1)} all-gather(f32[1024]{0:T(1024)S(1)} %broadcast_divide_fusion), channel_id=1, replica_groups=mesh['wake'=16,'col'=2] {'wake'}, dimensions={0}, use_global_device_ids=true | all-gather | bytes 69632 | tf_op jit(solution)/shard_map/all_gather | solution.py:117
  1301.9 36.8 %psum.102 = f32[6]{0:T(128)S(1)} all-reduce(f32[6]{0:T(128)S(1)} %stack.103), channel_id=1, replica_groups=mesh['wake'=16,'col'=2] {'wake','col'}, use_global_device_ids=true, to_apply=%region_55.0 | all-reduce | flops 6 | bytes 48 | tf_op jit(solution)/shard_map/psum | solution.py:132
  1344.6 41.6 %psum.103 = f32[]{:T(128)} all-reduce(f32[]{:T(128)} %multiply_reduce_fusion.3), channel_id=1, replica_groups=mesh['wake'=16,'col'=2] {'wake','col'}, use_global_device_ids=true, to_apply=%region_57.0 | all-reduce | flops 1 | bytes 8 | tf_op jit(solution)/shard_map/psum | solution.py:136
  (358 shorter events, 488.8 us)
Async XLA Ops:
  0.6 710.9 %copy-start = (f32[1,32,16384]{2,1,0:T(8,128)S(1)}, f32[1,32,16384]{2,1,0:T(8,128)}, u32[]{:S(2)}) copy-start(f32[1,32,16384]{2,1,0:T(8,128)} %param.47) | copy-start | bytes 6291460
  3.5 11.7 collective-permute-start
  44.7 665.1 %copy-start.1 = (f32[16,1,1,128,128]{4,3,2,1,0:T(8,128)S(1)}, f32[16,1,1,128,128]{4,3,2,1,0:T(8,128)}, u32[]{:S(2)}) copy-start(f32[16,1,1,128,128]{4,3,2,1,0:T(8,128)} %param.44) | copy-start | bytes 3145732
  45.6 10.0 copy-start.3
  64.4 10.0 copy-start.3
  83.3 10.0 copy-start.3
  102.1 10.0 copy-start.3
  121.0 10.0 copy-start.3
  139.9 10.0 copy-start.3
  158.7 10.0 copy-start.3
  177.6 10.0 copy-start.3
  196.4 10.0 copy-start.3
  215.3 10.0 copy-start.3
  234.2 10.0 copy-start.3
  253.0 10.0 copy-start.3
  271.9 10.0 copy-start.3
  290.7 10.0 copy-start.3
  309.6 10.0 copy-start.3
  328.4 10.0 copy-start.3
  347.3 10.0 copy-start.3
  366.2 10.0 copy-start.3
  385.0 10.0 copy-start.3
  403.9 10.0 copy-start.3
  422.7 10.0 copy-start.3
  441.6 10.0 copy-start.3
  460.5 10.0 copy-start.3
  479.3 10.0 copy-start.3
  498.2 10.0 copy-start.3
  517.0 10.0 copy-start.3
  535.9 10.0 copy-start.3
  554.8 10.0 copy-start.3
  573.6 10.0 copy-start.3
  592.5 10.0 copy-start.3
  611.3 10.0 copy-start.3
  630.2 10.0 copy-start.3
  648.2 65.1 %copy-start.2 = (f32[1,32,2048]{2,1,0:T(8,128)S(1)}, f32[1,32,2048]{2,1,0:T(8,128)}, u32[]{:S(2)}) copy-start(f32[1,32,2048]{2,1,0:T(8,128)} %param.46) | copy-start | bytes 786436
  648.2 70.4 %copy-start.4 = (f32[1024]{0:T(1024)S(1)}, f32[1024]{0:T(1024)}, u32[]{:S(2)}) copy-start(f32[1024]{0:T(1024)} %param.43) | copy-start | bytes 12292
where the time goes:
time: 1450 us; the launch traced here: 1430 us
  blocking collectives  693 us (48%)
  other arithmetic  598 us (41%)
  local copies, waits for them, and re-layouts  85.1 us (6%)
  between operations  24.7 us (2%)
  matrix products  23.4 us (2%)
    reduce_sum x32, other arithmetic, induce(): near_len = jnp.sqrt(jnp.sum(near_arm * near_arm, axis=0))  295 us
    reduce_sum x32, other arithmetic, induce(): return jnp.sum(factor * normal_part, axis=1)  253 us
    psum x6, blocking collectives, body(): lax.psum(jnp.sum(remainder * remainder), ('wake', 'col'))  252 us
    psum x6, blocking collectives, body(): coeffs = lax.psum(local_dots, ('wake', 'col'))  221 us
    all_gather x6, blocking collectives, body(): column_vec = lax.all_gather(vector, 'wake', axis=0, tiled=True)  126 us
    psum x1, blocking collectives, body(): initial_sq = lax.psum(jnp.sum(right_side * right_side), ('wake', 'col'))  37.1 us
    unnamed x6, blocking collectives  30.1 us
  transfers between devices with their start and end apart: 1, of which 0 were waited for; matrix products, arithmetic and copies ran while one was open for 1% of the time, Pallas kernels for 0%

commit v1 on v0

v1 whole, which is shorter than its diff:
```python
import functools
import math

import jax
import jax.numpy as jnp
from jax import lax
from jax.experimental import pallas as pl
from jax.experimental.pallas import tpu as pltpu
from jax.sharding import PartitionSpec as P

KRYLOV = 6
CORE_SQ = 0.01
FOUR_PI = 4.0 * math.pi
LANES = 128
FEATURES = 48
PIECE_OF_PANEL = (0, 0, 1, 0, 2, 1)
PIECE_OF_SEGMENT = (0, 1, 0, 2, 0, 1)
PANEL_STEP = 64
NODE_STEP = 16

VMEM = pl.BlockSpec(memory_space=pltpu.VMEM)
SMEM = pl.BlockSpec(memory_space=pltpu.SMEM)


def three_pieces(value):
    high = value.astype(jnp.bfloat16).astype(jnp.float32)
    rest = value - high
    middle = rest.astype(jnp.bfloat16).astype(jnp.float32)
    low = (rest - middle).astype(jnp.bfloat16).astype(jnp.float32)
    return high, middle, low


def pack_kernel(nodes_ref, circulation_ref, filament_ref, out_ref):
    copies, _, rows, _ = out_ref.shape
    own = [
        jnp.concatenate([nodes_ref[q : q + 1, r * LANES : (r + 1) * LANES] for r in range(rows)], axis=0)
        for q in range(3)
    ]
    own.append(circulation_ref[...])
    own.append(filament_ref[...].astype(jnp.float32) + 1.0)
    for q in range(5):
        for k in range(copies):
            out_ref[k, q] = own[q]


def pack_nodes(wake_nodes, circulation, filament, copies):
    rows = circulation.shape[0] // LANES
    return pl.pallas_call(
        pack_kernel,
        out_shape=jax.ShapeDtypeStruct((copies, 5, rows, LANES), jnp.float32),
        in_specs=[VMEM, VMEM, VMEM],
        out_specs=VMEM,
        name="pack_nodes",
    )(wake_nodes, circulation.reshape(rows, LANES), filament.reshape(rows, LANES))


def induce_kernel(
    nodes_ref, points_ref, normals_ref, stream_ref, right_ref, copies_ref,
    row_ref, feature_ref, feature_bf_ref, panel_ref, panel_bf_ref, total_ref,
):
    rows = nodes_ref.shape[0] * nodes_ref.shape[2]
    x, y, z, circulation, tag = [nodes_ref[:, q].reshape(rows, LANES) for q in range(5)]
    piece_rows = right_ref.shape[0]

    def spread(ref, q):
        return jnp.concatenate(
            [ref[q : q + 1, r * LANES : (r + 1) * LANES] for r in range(piece_rows)], axis=0
        )

    points = [spread(points_ref, q) for q in range(3)]
    normals = [spread(normals_ref, q) for q in range(3)]
    middle = [0.5 * (jnp.max(p, keepdims=True) + jnp.min(p, keepdims=True)) for p in points]

    px, py, pz = [points[q] - middle[q] for q in range(3)]
    panel_features = [
        normals[1] * pz - normals[2] * py,
        normals[2] * px - normals[0] * pz,
        normals[0] * py - normals[1] * px,
        normals[0], normals[1], normals[2],
    ]
    panel_pieces = [three_pieces(feature) for feature in panel_features]
    for r in range(piece_rows):
        own = slice(r * LANES, (r + 1) * LANES)
        for q in range(3):
            panel_ref[q, own, :] = jnp.broadcast_to(points[q][r : r + 1, :], (LANES, LANES)).T
        stack = jnp.concatenate(
            [panel_pieces[k][p][r : r + 1, :] for p in PIECE_OF_PANEL for k in range(6)]
            + [jnp.zeros((LANES - 36, LANES), jnp.float32)],
            axis=0,
        )
        panel_bf_ref[own, :] = stack.T[:, :FEATURES].astype(jnp.bfloat16)

    lane = lax.broadcasted_iota(jnp.int32, (rows, LANES), 1)
    row = lax.broadcasted_iota(jnp.int32, (rows, LANES), 0)

    def following(value):
        turned = pltpu.roll(value, LANES - 1, 1)
        return jnp.where(lane == LANES - 1, pltpu.roll(turned, rows - 1, 0), turned)

    nx, ny, nz, next_tag = [following(value) for value in (x, y, z, tag)]
    linked = (tag == next_tag) & ((lane < LANES - 1) | (row < rows - 1))
    strength = jnp.where(linked, circulation * (1.0 / FOUR_PI), 0.0)
    ex, ey, ez = x - nx, y - ny, z - nz
    ax, ay, az = x - middle[0], y - middle[1], z - middle[2]
    bx, by, bz = nx - middle[0], ny - middle[1], nz - middle[2]
    segment_features = [
        strength * ex, strength * ey, strength * ez,
        strength * (ay * bz - az * by),
        strength * (az * bx - ax * bz),
        strength * (ax * by - ay * bx),
    ]
    total_ref[...] = jnp.zeros_like(total_ref)
    feature_ref[...] = jnp.zeros_like(feature_ref)
    for group in range(rows // LANES):
        own = slice(group * LANES, (group + 1) * LANES)
        for q, value in enumerate((x, y, z)):
            row_ref[q, 0:LANES, :] = value[own].T
        for q, value in enumerate((nx, ny, nz)):
            row_ref[q, LANES : LANES + 8, :] = jnp.broadcast_to(value[own].T[LANES - 1 : LANES], (8, LANES))
        for k in range(6):
            pieces = three_pieces(segment_features[k][own].T)
            for p in range(6):
                feature_ref[pl.ds(p * 6 + k, LANES, stride=FEATURES), :] = pieces[PIECE_OF_SEGMENT[p]]

        def narrow(i, carry):
            part = pl.ds(pl.multiple_of(i * FEATURES, FEATURES), FEATURES)
            feature_bf_ref[part, :] = feature_ref[part, :].astype(jnp.bfloat16)
            return carry

        lax.fori_loop(0, LANES, narrow, 0, unroll=8)

        def arms(panel, t):
            rx, ry, rz = [panel[q] - row_ref[q, pl.ds(t, 1), :] for q in range(3)]
            square = rx * rx + ry * ry + rz * rz
            return rx, ry, rz, square * lax.rsqrt(jnp.maximum(square, 1e-36))

        def panel_step(b, carry):
            part = pl.ds(pl.multiple_of(b * PANEL_STEP, PANEL_STEP), PANEL_STEP)
            panel = [panel_ref[q, part, :] for q in range(3)]
            features = panel_bf_ref[part, :]

            def node_step(block, state):
                (rx, ry, rz, length), total = state
                first = pl.multiple_of(block * NODE_STEP, NODE_STEP)
                base = pl.multiple_of(first * FEATURES, FEATURES)
                for k in range(NODE_STEP):
                    normal_part = jnp.dot(
                        features,
                        feature_bf_ref[pl.ds(base + k * FEATURES, FEATURES), :],
                        preferred_element_type=jnp.float32,
                    )
                    sx, sy, sz, after = arms(panel, first + k + 1)
                    product = length * after
                    inner = rx * sx + ry * sy + rz * sz
                    below = product * (product + inner) + CORE_SQ
                    total = total + ((length + after) * normal_part) * pl.reciprocal(below)
                    rx, ry, rz, length = sx, sy, sz, after
                return (rx, ry, rz, length), total

            start = (arms(panel, 0), jnp.zeros((PANEL_STEP, LANES), jnp.float32))
            _, total = lax.fori_loop(0, LANES // NODE_STEP, node_step, start)
            total_ref[part, :] += total
            return carry

        lax.fori_loop(0, piece_rows * LANES // PANEL_STEP, panel_step, 0)

    onset = stream_ref[0] * normals[0] + stream_ref[1] * normals[1] + stream_ref[2] * normals[2]
    for r in range(piece_rows):
        induced = jnp.sum(total_ref[r * LANES : (r + 1) * LANES, :].T, axis=0, keepdims=True)
        right_ref[r : r + 1, :] = -(onset[r : r + 1, :] + induced)
    right = right_ref[...]
    for k in range(copies_ref.shape[0]):
        copies_ref[k] = right


def induce(nodes, points, normals, freestream, copies):
    piece = points.shape[1]
    piece_rows = piece // LANES
    pairs = piece * nodes.size // 5
    return pl.pallas_call(
        induce_kernel,
        out_shape=(
            jax.ShapeDtypeStruct((piece_rows, LANES), jnp.float32),
            jax.ShapeDtypeStruct((copies, piece_rows, LANES), jnp.float32),
        ),
        in_specs=[VMEM, VMEM, VMEM, SMEM],
        out_specs=(VMEM, VMEM),
        scratch_shapes=[
            pltpu.VMEM((3, LANES + 8, LANES), jnp.float32),
            pltpu.VMEM((LANES * FEATURES, LANES), jnp.float32),
            pltpu.VMEM((LANES * FEATURES, LANES), jnp.bfloat16),
            pltpu.VMEM((3, piece, LANES), jnp.float32),
            pltpu.VMEM((piece, FEATURES), jnp.bfloat16),
            pltpu.VMEM((piece, LANES), jnp.float32),
        ],
        compiler_params=pltpu.CompilerParams(vmem_limit_bytes=24 * 2**20),
        cost_estimate=pl.CostEstimate(flops=30 * pairs, bytes_accessed=2**21, transcendentals=2 * pairs),
        name="induce",
    )(nodes, points, normals, freestream)


def whole_sum(value):
    return jnp.sum(value, keepdims=True)


def orthogonalize(image_ref, known_refs, column_ref):
    image = image_ref[...].reshape(-1, LANES)
    known = [ref[...] for ref in known_refs]
    coeffs = [whole_sum(image * member) for member in known]
    for coeff, member in zip(coeffs, known):
        image = image - coeff * member
    norm = jnp.sqrt(whole_sum(image * image))
    for i, value in enumerate(coeffs + [norm]):
        column_ref[i : i + 1, :] = jnp.broadcast_to(value, (1, LANES))
    return image / norm


def step_kernel(known_count, n_col, *refs):
    place_ref, index_refs, refs = refs[0], refs[1 : 1 + n_col], refs[1 + n_col :]
    image_ref, known_refs, refs = refs[0], refs[1 : 1 + known_count], refs[1 + known_count :]
    self_ref, refs = refs[0], refs[1:]
    near_refs, left_refs, right_refs = refs[:n_col], refs[n_col : 2 * n_col], refs[2 * n_col : 3 * n_col]
    vector_ref, column_ref, copies_ref = refs[3 * n_col :]
    piece_rows = self_ref.shape[0]
    piece = piece_rows * LANES
    rank = right_refs[0].shape[0]
    n_wake = right_refs[0].shape[1] // piece
    vector_ref[...] = orthogonalize(image_ref, known_refs, column_ref)
    place, mine = place_ref[0], place_ref[1]

    far = jnp.zeros((rank, piece), jnp.float32)
    near = [jnp.zeros((LANES, LANES), jnp.float32) for _ in range(piece_rows)]
    for shift in range(n_col):
        group = lax.rem(mine - shift + n_col, n_col)

        def chunk(w, total):
            first = (w * n_col + group) * piece_rows
            for r in range(piece_rows):
                entries = vector_ref[pl.ds(first + r, 1), :]
                columns = pl.ds(pl.multiple_of(w * piece, LANES) + r * LANES, LANES)
                total = total + right_refs[shift][:, columns] * entries
            return total

        coeff = lax.fori_loop(0, n_wake, chunk, jnp.zeros((rank, LANES), jnp.float32), unroll=4)
        coeff = jnp.sum(coeff, axis=1, keepdims=True)
        if shift == 0:
            left = left_refs[0][:, pl.ds(pl.multiple_of(mine * piece, LANES), piece)]
        else:
            left = left_refs[shift][...]
        far = far + left * coeff
        for r in range(piece_rows):
            if shift == 0:
                row_block = mine * piece_rows + r
            else:
                row_block = r
            block = index_refs[shift][row_block if shift == 0 else r]
            where = (lax.div(block, piece_rows) * n_col + group) * piece_rows + lax.rem(block, piece_rows)
            near[r] = near[r] + near_refs[shift][row_block] * vector_ref[pl.ds(where, 1), :]
    far = jnp.sum(far, axis=0, keepdims=True)
    out_rows = []
    for r in range(piece_rows):
        out_rows.append(
            jnp.sum(near[r].T, axis=0, keepdims=True) + far[:, r * LANES : (r + 1) * LANES]
        )
    own = vector_ref[pl.ds(pl.multiple_of(place * piece_rows, piece_rows), piece_rows), :]
    image = self_ref[...] * own + jnp.concatenate(out_rows, axis=0)
    for k in range(copies_ref.shape[0]):
        copies_ref[k] = image


def arnoldi_step(place, indices, image, known, self_term, nears, lefts, rights):
    n_col = len(nears)
    copies, piece_rows, _ = image.shape
    total_rows = copies * piece_rows
    operands = [image, *known, self_term, *nears, *lefts, *rights]
    return pl.pallas_call(
        functools.partial(step_kernel, len(known), n_col),
        out_shape=(
            jax.ShapeDtypeStruct((total_rows, LANES), jnp.float32),
            jax.ShapeDtypeStruct((8, LANES), jnp.float32),
            jax.ShapeDtypeStruct((copies, piece_rows, LANES), jnp.float32),
        ),
        in_specs=[SMEM] * (1 + n_col) + [VMEM] * len(operands),
        out_specs=(VMEM, VMEM, VMEM),
        compiler_params=pltpu.CompilerParams(vmem_limit_bytes=32 * 2**20),
        name="arnoldi_step",
    )(place, *indices, *operands)


def small_solve(gram_matrix, projected):
    size_now = len(projected)
    factor = [[None for inner_pos in range(size_now)] for outer_pos in range(size_now)]
    for outer_pos in range(size_now):
        for inner_pos in range(outer_pos + 1):
            partial_sum = gram_matrix[outer_pos][inner_pos]
            for middle in range(inner_pos):
                partial_sum = partial_sum - factor[outer_pos][middle] * factor[inner_pos][middle]
            if inner_pos == outer_pos:
                factor[outer_pos][inner_pos] = jnp.sqrt(partial_sum)
            else:
                factor[outer_pos][inner_pos] = partial_sum / factor[inner_pos][inner_pos]
    forward = []
    for outer_pos in range(size_now):
        partial_sum = projected[outer_pos]
        for middle in range(outer_pos):
            partial_sum = partial_sum - factor[outer_pos][middle] * forward[middle]
        forward.append(partial_sum / factor[outer_pos][outer_pos])
    backward = [None for outer_pos in range(size_now)]
    for outer_pos in reversed(range(size_now)):
        partial_sum = forward[outer_pos]
        for middle in range(outer_pos + 1, size_now):
            partial_sum = partial_sum - factor[middle][outer_pos] * backward[middle]
        backward[outer_pos] = partial_sum / factor[outer_pos][outer_pos]
    return backward


def finish_kernel(place_ref, image_ref, *refs):
    known_refs, column_refs, out_ref, last_ref = refs[:KRYLOV], refs[KRYLOV : 2 * KRYLOV], refs[-2], refs[-1]
    orthogonalize(image_ref, known_refs, last_ref)
    norm = column_refs[0][0:1, :]
    columns = []
    for column, ref in enumerate(list(column_refs[1:]) + [last_ref]):
        columns.append([ref[i : i + 1, :] for i in range(column + 2)])
    gram = [
        [sum(columns[i][k] * columns[j][k] for k in range(j + 2)) for j in range(i + 1)]
        for i in range(KRYLOV)
    ]
    combination = small_solve(gram, [norm * columns[j][0] for j in range(KRYLOV)])
    piece_rows = out_ref.shape[0]
    part = pl.ds(pl.multiple_of(place_ref[0] * piece_rows, piece_rows), piece_rows)
    strengths = combination[0] * known_refs[0][part, :]
    for position in range(1, KRYLOV):
        strengths = strengths + combination[position] * known_refs[position][part, :]
    out_ref[...] = strengths


def finish(place, image, known, columns):
    piece_rows = image.shape[1]
    return pl.pallas_call(
        finish_kernel,
        out_shape=jax.ShapeDtypeStruct((piece_rows, LANES), jnp.float32),
        in_specs=[SMEM] + [VMEM] * (1 + len(known) + len(columns)),
        out_specs=VMEM,
        scratch_shapes=[pltpu.VMEM((8, LANES), jnp.float32)],
        compiler_params=pltpu.CompilerParams(vmem_limit_bytes=16 * 2**20),
        name="finish",
    )(place, image, *known, *columns)


def body(
    points,
    normals,
    freestream,
    wake_nodes,
    circulation,
    filament,
    self_term,
    near_blocks,
    near_index,
    far_left,
    far_right,
):
    everyone = ("wake", "col")
    n_wake, n_col = lax.axis_size("wake"), lax.axis_size("col")
    copies = n_wake * n_col
    piece = points.shape[1]
    piece_rows = piece // LANES
    mine = lax.axis_index("col")
    place = jnp.stack([lax.axis_index("wake") * n_col + mine, mine])

    near_own, index_own = near_blocks[:, 0, 0], near_index[:, 0, 0]
    left_own, right_own = far_left[0], far_right[0]
    nears, indices, lefts, rights = [near_own], [index_own], [left_own], [right_own]
    for shift in range(1, n_col):
        pairs = [(source, (source + shift) % n_col) for source in range(n_col)]
        target = lax.rem(mine + shift, n_col)
        index_part = lax.dynamic_slice_in_dim(index_own, target * piece_rows, piece_rows, 0).astype(jnp.float32)
        nears.append(
            lax.ppermute(lax.dynamic_slice_in_dim(near_own, target * piece_rows, piece_rows, 0), "col", pairs)
        )
        indices.append(lax.ppermute(index_part, "col", pairs).astype(jnp.int32))
        lefts.append(lax.ppermute(lax.dynamic_slice_in_dim(left_own, target * piece, piece, 1), "col", pairs))
        rights.append(lax.ppermute(right_own, "col", pairs))

    packed = pack_nodes(wake_nodes, circulation, filament, n_wake)
    nodes = lax.all_to_all(packed, "wake", 0, 0, tiled=True)
    right_side, image_copies = induce(nodes, points, normals, freestream, copies)
    own_self = self_term.reshape(piece_rows, LANES)
    known, columns = [], []
    for _ in range(KRYLOV):
        image = lax.all_to_all(image_copies, everyone, 0, 0, tiled=True)
        vector, column, image_copies = arnoldi_step(
            place, indices, image, known, own_self, nears, lefts, rights
        )
        known.append(vector)
        columns.append(column)
    image = lax.all_to_all(image_copies, everyone, 0, 0, tiled=True)
    strengths = finish(place, image, known, columns)
    return right_side.reshape(piece), strengths.reshape(piece)


def solution(mesh):
    in_specs = (
        P(None, ("wake", "col")),
        P(None, ("wake", "col")),
        P(),
        P(None, "wake"),
        P("wake"),
        P("wake"),
        P(("wake", "col")),
        P("wake", "col", None, None, None),
        P("wake", "col", None),
        P("col", None, "wake"),
        P("wake", None, "col"),
    )
    out_specs = (P(("wake", "col")), P(("wake", "col")))
    return jax.shard_map(body, mesh=mesh, in_specs=in_specs, out_specs=out_specs, check_vma=False)
```

time: 1450 us -> 190 us (0.13); the launches traced: 1430 us -> 189 us
  blocking collectives: 693 us -> 64.6 us
  other arithmetic: 598 us -> 0.76 us
  Pallas kernels: 0 us -> 91.5 us
  local copies, waits for them, and re-layouts: 85.1 us -> 2.58 us
  between operations: 24.7 us -> 0.78 us
  matrix products: 23.4 us -> 0 us
    reduce_sum x77 -> x0, other arithmetic: 570 us -> none  [the longest x32 295 us: induce(): near_len = jnp.sqrt(jnp.sum(near_arm * near_arm, axis=0))]
    psum x13 -> x0, blocking collectives: 511 us -> none  [the longest x6 252 us: body(): lax.psum(jnp.sum(remainder * remainder), ('wake', 'col'))]
    all_gather x7 -> x0, blocking collectives: 152 us -> none  [the longest x6 126 us: body(): column_vec = lax.all_gather(vector, 'wake', axis=0, tiled=True)]
    pallas_call x0 -> x9, Pallas kernels: none -> 91.5 us  [the longest x1 70.1 us: induce(): pl.pallas_call(induce_kernel, out_shape=(jax.ShapeDtypeStruct((piece_rows...]
    all_to_all x0 -> x6, blocking collectives: none -> 64.6 us  [body(): image = lax.all_to_all(image_copies, everyone, 0, 0, tiled=True)]
    slice x109 -> x0, local copies, waits for them, and re-layouts: 61.5 us -> none  [the longest x32 27.9 us: induce(): far_arm = points[:, :, None] - segments[3:6, None, :]]
    unnamed x6 -> x0, blocking collectives: 30.1 us -> none
    dot_general x20 -> x0, matrix products: 23.4 us -> none  [the longest x6 10.5 us: body(): far_coeff = jnp.dot(right_factor, column_vec, precision=highest)]
  transfers between devices with their start and end apart: 1 -> 6, of which waited for: 0 -> 3; matrix products, arithmetic and copies ran while one was open for 1% -> 2% of each run, Pallas kernels for 0% -> 38%
where the time goes in v1:
time: 190 us; the launch traced here: 189 us
  Pallas kernels  91.5 us (48%)
  blocking collectives  64.6 us (34%)
  starting transfers between devices  14.8 us (8%)
  waiting for transfers between devices  13.8 us (7%)
  local copies, waits for them, and re-layouts  2.58 us (1%)
    pallas_call x1, Pallas kernels, induce(): pl.pallas_call(induce_kernel, out_shape=(jax.ShapeDtypeStruct((piece_rows...  70.1 us
    all_to_all x6, blocking collectives, body(): image = lax.all_to_all(image_copies, everyone, 0, 0, tiled=True)  64.6 us
    pallas_call x6, Pallas kernels, arnoldi_step(): pl.pallas_call(functools.partial(step_kernel, len(known), n_col), out_sha...  18.3 us
    all_to_all x1, waiting for transfers between devices, body(): nodes = lax.all_to_all(packed, 'wake', 0, 0, tiled=True)  8.71 us
    all_to_all x1, starting transfers between devices, body(): nodes = lax.all_to_all(packed, 'wake', 0, 0, tiled=True)  5.98 us
    ppermute x1, waiting for transfers between devices, body(): indices.append(lax.ppermute(index_part, 'col', pairs).astype(jnp.int32))  4.65 us
  transfers between devices with their start and end apart: 6, of which 3 were waited for; matrix products, arithmetic and copies ran while one was open for 2% of the time, Pallas kernels for 38%

profile of v1, /device:TPU:0, one launch (start us, length us, event | category | flops | bytes accessed | tf_op | source)
XLA Modules:
  0.0 188.9 jit_solution(16239035912857980527)
XLA Ops:
  0.6 0.0 copy-start.7
  0.6 0.0 copy-start.6
  0.7 0.0 copy-start.5
  0.7 3.0 %collective-permute-start.3 = (f32[32,16384]{1,0:T(8,128)}, f32[32,16384]{1,0:T(8,128)}, u32[]{:S(2)}, u32[]{:S(2)}) collective-permute-start(f32[32,16384]{1,0:T(8,128)} %bitcast.17), channel_id=1, source_target_pairs={{0,1},{1,0},{2,3},{3,2},{4,5},{5,4},{6,7},{7,6},{8,9},{9,8},{10,11... | collective-permute-start | bytes 6291464 | tf_op jit(solution)/shard_map/ppermute | solution.py:383
  3.7 1.5 pack_nodes.1
  5.2 6.0 %all-to-all-start = ((f32[16,5,8,128]{3,2,1,0:T(8,128)}), f32[16,5,8,128]{3,2,1,0:T(8,128)}, u32[]{:S(2)}, u32[]{:S(2)}) async-start(f32[16,5,8,128]{3,2,1,0:T(8,128)} %pack_nodes.1), calls=%async_computation | async-start | bytes 655360 | tf_op jit(solution)/shard_map/all_to_all | solution.py:386
  11.2 1.9 dynamic-slice_bitcast_fusion
  13.1 0.5 collective-permute-start.1
  13.6 0.0 copy-start.2
  13.6 0.0 copy-start.4
  13.6 0.0 copy-start
  13.6 0.0 copy-start.1
  13.6 0.0 copy-start.3
  13.6 8.7 %all-to-all-done.nodes_ref = f32[16,5,8,128]{3,2,1,0:T(8,128)} async-done(((f32[16,5,8,128]{3,2,1,0:T(8,128)}), f32[16,5,8,128]{3,2,1,0:T(8,128)}, u32[]{:S(2)}, u32[]{:S(2)}) %all-to-all-start) | async-done | bytes 327712 | tf_op jit(solution)/shard_map/all_to_all | solution.py:386
  22.3 0.0 copy-done.7
  22.3 0.0 copy-done.6
  22.3 0.0 copy-done.5
  22.3 70.1 %induce.1 = (f32[8,128]{1,0:T(8,128)}, f32[32,8,128]{2,1,0:T(8,128)}) custom-call(f32[16,5,8,128]{3,2,1,0:T(8,128)} %all-to-all-done.nodes_ref, f32[3,1024]{1,0:T(4,128)S(1)} %copy-done.5, f32[3,1024]{1,0:T(4,128)S(1)} %copy-done.6, f32[3]{0:T(128)S(1)} %copy-done.7), custom_call_target="tpu_custom_call" | custom-call | flops 503316480 | bytes 2097152 | tf_op jit(solution)/shard_map/induce/pallas_call | solution.py:180
  92.5 3.3 %all-to-all-start.1 = ((f32[32,8,128]{2,1,0:T(8,128)}), f32[32,8,128]{2,1,0:T(8,128)}, u32[]{:S(2)}, u32[]{:S(2)}) async-start(f32[32,8,128]{2,1,0:T(8,128)} %get-tuple-element.23), calls=%async_computation.1 | async-start | bytes 262144 | tf_op jit(solution)/shard_map/all_to_all | solution.py:391
  95.7 0.0 copy-done.2
  95.7 0.7 dynamic-slice_bitcast_fusion.1
  96.4 1.6 collective-permute-start.2
  98.0 0.0 copy-done.4
  98.0 0.1 fusion.1
  98.1 0.5 collective-permute-start
  98.5 0.1 pad_add_fusion.refs_0_.place_ref
  98.6 4.7 %collective-permute-done = f32[8]{0:T(128)} collective-permute-done((f32[8]{0:T(128)S(1)}, f32[8]{0:T(128)}, u32[]{:S(2)}, u32[]{:S(2)}) %collective-permute-start) | collective-permute-done | bytes 64 | tf_op jit(solution)/shard_map/ppermute | solution.py:381
  103.2 0.6 convert_element_type.11.refs_2_
  103.9 0.0 collective-permute-done.2.refs_8_.refs_9_.refs_10_.refs_11_.refs_12_.refs_13_
  103.9 0.0 collective-permute-done.1.refs_6_.refs_7_.refs_8_.refs_9_.refs_10_.refs_11_
  103.9 0.5 all-to-all-done.1.refs_3_
  104.3 0.0 collective-permute-done.3.refs_10_.refs_11_.refs_12_.refs_13_.refs_14_.refs_15_
  104.3 0.0 copy-done
  104.3 0.0 copy-done.1
  104.4 0.0 copy-done.3
  104.4 2.9 %arnoldi_step.6 = (f32[256,128]{1,0:T(8,128)S(1)}, f32[8,128]{1,0:T(8,128)S(1)}, f32[32,8,128]{2,1,0:T(8,128)S(1)}) custom-call(s32[2]{0:T(128)S(1)} %pad_add_fusion.refs_0_.place_ref, s32[16]{0:T(128)S(1)} %bitcast.42, s32[8]{0:T(128)S(1)} %convert_element_type.11.refs_2_, f32[32,8,128]{2,1,0:T(8,128)} %all-to-all-done.1.refs_3_, f32[8,128]{1,0:T(8,128)S(1)} %bitcast.36, ...), custom_call_target="tpu_custom_call" | custom-call | tf_op jit(solution)/shard_map/arnoldi_step/pallas_call | solution.py:276
  107.3 13.0 %all_to_all.40.refs_3_ = f32[32,8,128]{2,1,0:T(8,128)S(1)} all-to-all(f32[32,8,128]{2,1,0:T(8,128)S(1)} %get-tuple-element.24), channel_id=1, replica_groups=mesh['wake'=16,'col'=2] {'wake','col'}, dimensions={0} | all-to-all | bytes 262144 | tf_op jit(solution)/shard_map/all_to_all | solution.py:391
  120.3 3.0 %arnoldi_step.7 = (f32[256,128]{1,0:T(8,128)S(1)}, f32[8,128]{1,0:T(8,128)S(1)}, f32[32,8,128]{2,1,0:T(8,128)S(1)}) custom-call(s32[2]{0:T(128)S(1)} %pad_add_fusion.refs_0_.place_ref, s32[16]{0:T(128)S(1)} %bitcast.43, s32[8]{0:T(128)S(1)} %convert_element_type.11.refs_2_, f32[32,8,128]{2,1,0:T(8,128)S(1)} %all_to_all.40.refs_3_, ...), custom_call_target="tpu_custom_call" | custom-call | tf_op jit(solution)/shard_map/arnoldi_step/pallas_call | solution.py:276
  123.3 10.3 %all_to_all.41.refs_3_ = f32[32,8,128]{2,1,0:T(8,128)S(1)} all-to-all(f32[32,8,128]{2,1,0:T(8,128)S(1)} %get-tuple-element.26), channel_id=1, replica_groups=mesh['wake'=16,'col'=2] {'wake','col'}, dimensions={0} | all-to-all | bytes 262144 | tf_op jit(solution)/shard_map/all_to_all | solution.py:391
  133.6 3.1 %arnoldi_step.8 = (f32[256,128]{1,0:T(8,128)S(1)}, f32[8,128]{1,0:T(8,128)S(1)}, f32[32,8,128]{2,1,0:T(8,128)S(1)}) custom-call(s32[2]{0:T(128)S(1)} %pad_add_fusion.refs_0_.place_ref, s32[16]{0:T(128)S(1)} %bitcast.44, s32[8]{0:T(128)S(1)} %convert_element_type.11.refs_2_, f32[32,8,128]{2,1,0:T(8,128)S(1)} %all_to_all.41.refs_3_, ...), custom_call_target="tpu_custom_call" | custom-call | tf_op jit(solution)/shard_map/arnoldi_step/pallas_call | solution.py:276
  136.7 10.3 %all_to_all.42.refs_3_ = f32[32,8,128]{2,1,0:T(8,128)S(1)} all-to-all(f32[32,8,128]{2,1,0:T(8,128)S(1)} %get-tuple-element.28), channel_id=1, replica_groups=mesh['wake'=16,'col'=2] {'wake','col'}, dimensions={0} | all-to-all | bytes 262144 | tf_op jit(solution)/shard_map/all_to_all | solution.py:391
  147.0 3.1 %arnoldi_step.9 = (f32[256,128]{1,0:T(8,128)S(1)}, f32[8,128]{1,0:T(8,128)S(1)}, f32[32,8,128]{2,1,0:T(8,128)S(1)}) custom-call(s32[2]{0:T(128)S(1)} %pad_add_fusion.refs_0_.place_ref, s32[16]{0:T(128)S(1)} %bitcast.45, s32[8]{0:T(128)S(1)} %convert_element_type.11.refs_2_, f32[32,8,128]{2,1,0:T(8,128)S(1)} %all_to_all.42.refs_3_, ...), custom_call_target="tpu_custom_call" | custom-call | tf_op jit(solution)/shard_map/arnoldi_step/pallas_call | solution.py:276
  150.1 10.3 %all_to_all.43.refs_3_ = f32[32,8,128]{2,1,0:T(8,128)S(1)} all-to-all(f32[32,8,128]{2,1,0:T(8,128)S(1)} %get-tuple-element.30), channel_id=1, replica_groups=mesh['wake'=16,'col'=2] {'wake','col'}, dimensions={0} | all-to-all | bytes 262144 | tf_op jit(solution)/shard_map/all_to_all | solution.py:391
  160.4 3.1 %arnoldi_step.10 = (f32[256,128]{1,0:T(8,128)S(1)}, f32[8,128]{1,0:T(8,128)S(1)}, f32[32,8,128]{2,1,0:T(8,128)S(1)}) custom-call(s32[2]{0:T(128)S(1)} %pad_add_fusion.refs_0_.place_ref, s32[16]{0:T(128)S(1)} %bitcast.46, s32[8]{0:T(128)S(1)} %convert_element_type.11.refs_2_, f32[32,8,128]{2,1,0:T(8,128)S(1)} %all_to_all.43.refs_3_, ...), custom_call_target="tpu_custom_call" | custom-call | tf_op jit(solution)/shard_map/arnoldi_step/pallas_call | solution.py:276
  163.6 10.3 %all_to_all.44.refs_3_ = f32[32,8,128]{2,1,0:T(8,128)S(1)} all-to-all(f32[32,8,128]{2,1,0:T(8,128)S(1)} %get-tuple-element.32), channel_id=1, replica_groups=mesh['wake'=16,'col'=2] {'wake','col'}, dimensions={0} | all-to-all | bytes 262144 | tf_op jit(solution)/shard_map/all_to_all | solution.py:391
  173.9 3.1 %arnoldi_step.11 = (f32[256,128]{1,0:T(8,128)S(1)}, f32[8,128]{1,0:T(8,128)S(1)}, f32[32,8,128]{2,1,0:T(8,128)S(1)}) custom-call(s32[2]{0:T(128)S(1)} %pad_add_fusion.refs_0_.place_ref, s32[16]{0:T(128)S(1)} %bitcast.47, s32[8]{0:T(128)S(1)} %convert_element_type.11.refs_2_, f32[32,8,128]{2,1,0:T(8,128)S(1)} %all_to_all.44.refs_3_, ...), custom_call_target="tpu_custom_call" | custom-call | tf_op jit(solution)/shard_map/arnoldi_step/pallas_call | solution.py:276
  177.0 10.3 %all_to_all.45.image_ref = f32[32,8,128]{2,1,0:T(8,128)S(1)} all-to-all(f32[32,8,128]{2,1,0:T(8,128)S(1)} %get-tuple-element.34), channel_id=1, replica_groups=mesh['wake'=16,'col'=2] {'wake','col'}, dimensions={0} | all-to-all | bytes 262144 | tf_op jit(solution)/shard_map/all_to_all | solution.py:397
  187.3 1.6 finish.1
Async XLA Ops:
  0.6 21.7 %copy-start.7 = (f32[3]{0:T(128)S(1)}, f32[3]{0:T(128)}, u32[]{:S(2)}) copy-start(f32[3]{0:T(128)} %stream_ref.1) | copy-start | bytes 40
  0.6 21.7 %copy-start.6 = (f32[3,1024]{1,0:T(4,128)S(1)}, f32[3,1024]{1,0:T(4,128)}, u32[]{:S(2)}) copy-start(f32[3,1024]{1,0:T(4,128)} %normals_ref.1) | copy-start | bytes 36868
  0.7 21.7 %copy-start.5 = (f32[3,1024]{1,0:T(4,128)S(1)}, f32[3,1024]{1,0:T(4,128)}, u32[]{:S(2)}) copy-start(f32[3,1024]{1,0:T(4,128)} %points_ref.1) | copy-start | bytes 36868
  0.7 103.7 %collective-permute-start.3 = (f32[32,16384]{1,0:T(8,128)}, f32[32,16384]{1,0:T(8,128)}, u32[]{:S(2)}, u32[]{:S(2)}) collective-permute-start(f32[32,16384]{1,0:T(8,128)} %bitcast.17), channel_id=1, source_target_pairs={{0,1},{1,0},{2,3},{3,2},{4,5},{5,4},{6,7},{7,6},{8,9},{9,8},{10,11... | collective-permute-start | bytes 6291464 | tf_op jit(solution)/shard_map/ppermute | solution.py:383
  5.2 17.2 %all-to-all-start = ((f32[16,5,8,128]{3,2,1,0:T(8,128)}), f32[16,5,8,128]{3,2,1,0:T(8,128)}, u32[]{:S(2)}, u32[]{:S(2)}) async-start(f32[16,5,8,128]{3,2,1,0:T(8,128)} %pack_nodes.1), calls=%async_computation | async-start | bytes 655360 | tf_op jit(solution)/shard_map/all_to_all | solution.py:386
  13.1 90.8 %collective-permute-start.1 = (f32[8,128,128]{2,1,0:T(8,128)}, f32[8,128,128]{2,1,0:T(8,128)}, u32[]{:S(2)}, u32[]{:S(2)}) collective-permute-start(f32[8,128,128]{2,1,0:T(8,128)} %dynamic-slice_bitcast_fusion), channel_id=1, source_target_pairs={{0,1},{1,0},{2,3},{3,2},{4,5},{5,4},{6,7},{7,6},{8,9},{9,8},{10,11... | collective-permute-start | bytes 1572872 | tf_op jit(solution)/shard_map/ppermute | solution.py:379
  13.6 82.1 %copy-start.2 = (f32[1,32,2048]{2,1,0:T(8,128)S(1)}, f32[1,32,2048]{2,1,0:T(8,128)}, u32[]{:S(2)}) copy-start(f32[1,32,2048]{2,1,0:T(8,128)} %param.20) | copy-start | bytes 786436
  13.6 84.4 %copy-start.4 = (s32[16,1,1]{0,2,1:T(1,128)S(1)}, s32[16,1,1]{0,2,1:T(1,128)}, u32[]{:S(2)}) copy-start(s32[16,1,1]{0,2,1:T(1,128)} %param.19) | copy-start | bytes 196
  13.6 90.7 %copy-start = (f32[1,32,16384]{2,1,0:T(8,128)S(1)}, f32[1,32,16384]{2,1,0:T(8,128)}, u32[]{:S(2)}) copy-start(f32[1,32,16384]{2,1,0:T(8,128)} %param.21) | copy-start | bytes 6291460
  13.6 90.7 %copy-start.1 = (f32[16,1,1,128,128]{4,3,2,1,0:T(8,128)S(1)}, f32[16,1,1,128,128]{4,3,2,1,0:T(8,128)}, u32[]{:S(2)}) copy-start(f32[16,1,1,128,128]{4,3,2,1,0:T(8,128)} %param.18) | copy-start | bytes 3145732
  13.6 90.7 %copy-start.3 = (f32[1024]{0:T(1024)S(1)}, f32[1024]{0:T(1024)}, u32[]{:S(2)}) copy-start(f32[1024]{0:T(1024)} %param.17) | copy-start | bytes 12292
  92.5 11.9 %all-to-all-start.1 = ((f32[32,8,128]{2,1,0:T(8,128)}), f32[32,8,128]{2,1,0:T(8,128)}, u32[]{:S(2)}, u32[]{:S(2)}) async-start(f32[32,8,128]{2,1,0:T(8,128)} %get-tuple-element.23), calls=%async_computation.1 | async-start | bytes 262144 | tf_op jit(solution)/shard_map/all_to_all | solution.py:391
  96.4 7.4 %collective-permute-start.2 = (f32[32,1024]{1,0:T(8,128)}, f32[32,1024]{1,0:T(8,128)S(1)}, u32[]{:S(2)}, u32[]{:S(2)}) collective-permute-start(f32[32,1024]{1,0:T(8,128)} %dynamic-slice_bitcast_fusion.1), channel_id=1, source_target_pairs={{0,1},{1,0},{2,3},{3,2},{4,5},{5,4},{6,7},{7,6},{8,9},{9,8},{10,11... | collective-permute-start | bytes 393224 | tf_op jit(solution)/shard_map/ppermute | solution.py:382
  98.1 5.2 %collective-permute-start = (f32[8]{0:T(128)S(1)}, f32[8]{0:T(128)}, u32[]{:S(2)}, u32[]{:S(2)}) collective-permute-start(f32[8]{0:T(128)S(1)} %fusion.1), channel_id=1, source_target_pairs={{0,1},{1,0},{2,3},{3,2},{4,5},{5,4},{6,7},{7,6},{8,9},{9,8},{10,11... | collective-permute-start | bytes 104 | tf_op jit(solution)/shard_map/ppermute | solution.py:381

commit v2 on v1

v2 whole, which is shorter than its diff:
```python
import functools
import math

import jax
import jax.numpy as jnp
from jax import lax
from jax.experimental import pallas as pl
from jax.experimental.pallas import tpu as pltpu
from jax.sharding import PartitionSpec as P

KRYLOV = 6
CORE_SQ = 0.01
FOUR_PI = 4.0 * math.pi
LANES = 128
PIECE_OF_PANEL = (0, 0, 1, 0, 2, 1)
PIECE_OF_SEGMENT = (0, 1, 0, 2, 0, 1)
NORMAL_ROWS = 48
LENGTH_ROWS = 32
WIDE = 2 * LANES
HALF = LANES // 2
PANEL_STEP = 128
NODE_STEP = 32

VMEM = pl.BlockSpec(memory_space=pltpu.VMEM)
SMEM = pl.BlockSpec(memory_space=pltpu.SMEM)


def pack_kernel(nodes_ref, circulation_ref, filament_ref, out_ref):
    copies, _, rows, _ = out_ref.shape
    own = [
        jnp.concatenate([nodes_ref[q : q + 1, r * LANES : (r + 1) * LANES] for r in range(rows)], axis=0)
        for q in range(3)
    ]
    own.append(circulation_ref[...])
    own.append(filament_ref[...].astype(jnp.float32) + 1.0)
    for q in range(5):
        for k in range(copies):
            out_ref[k, q] = own[q]


def pack_nodes(wake_nodes, circulation, filament, copies):
    rows = circulation.shape[0] // LANES
    return pl.pallas_call(
        pack_kernel,
        out_shape=jax.ShapeDtypeStruct((copies, 5, rows, LANES), jnp.float32),
        in_specs=[VMEM, VMEM, VMEM],
        out_specs=VMEM,
        name="pack_nodes",
    )(wake_nodes, circulation.reshape(rows, LANES), filament.reshape(rows, LANES))


def three_pieces(value):
    high = value.astype(jnp.bfloat16).astype(jnp.float32)
    rest = value - high
    middle = rest.astype(jnp.bfloat16).astype(jnp.float32)
    low = (rest - middle).astype(jnp.bfloat16).astype(jnp.float32)
    return high, middle, low


def panels_kernel(points_ref, normals_ref, stream_ref, normal_side_ref, length_side_ref, onset_ref, middle_ref):
    piece_rows = onset_ref.shape[0]

    def spread(ref, q):
        return jnp.concatenate(
            [ref[q : q + 1, r * LANES : (r + 1) * LANES] for r in range(piece_rows)], axis=0
        )

    points = [spread(points_ref, q) for q in range(3)]
    normals = [spread(normals_ref, q) for q in range(3)]
    middle = [0.5 * (jnp.max(p, keepdims=True) + jnp.min(p, keepdims=True)) for p in points]
    for q in range(3):
        middle_ref[q : q + 1, :] = jnp.broadcast_to(middle[q], (1, LANES))
    px, py, pz = [points[q] - middle[q] for q in range(3)]
    features = [
        normals[1] * pz - normals[2] * py,
        normals[2] * px - normals[0] * pz,
        normals[0] * py - normals[1] * px,
        normals[0], normals[1], normals[2],
    ]
    pieces = [three_pieces(feature) for feature in features]
    side = [pieces[k][p] for p in PIECE_OF_PANEL for k in range(6)]
    side += [jnp.zeros_like(px)] * (NORMAL_ROWS - len(side))
    pieces = [three_pieces(value) for value in (px, py, pz)]
    side += [pieces[k][p] for p in PIECE_OF_PANEL for k in range(3)]
    side += list(three_pieces(px * px + py * py + pz * pz)) + [jnp.ones_like(px)] * 3
    side += [jnp.zeros_like(px)] * (LANES - len(side))
    for r in range(piece_rows):
        own = slice(r * LANES, (r + 1) * LANES)
        turned = jnp.concatenate([value[r : r + 1, :] for value in side], axis=0).T
        normal_side_ref[own, :] = turned[:, :NORMAL_ROWS].astype(jnp.bfloat16)
        length_side_ref[own, :] = turned[:, NORMAL_ROWS : NORMAL_ROWS + LENGTH_ROWS].astype(jnp.bfloat16)
    onset_ref[...] = stream_ref[0] * normals[0] + stream_ref[1] * normals[1] + stream_ref[2] * normals[2]


def prepare_panels(points, normals, freestream):
    piece = points.shape[1]
    return pl.pallas_call(
        panels_kernel,
        out_shape=(
            jax.ShapeDtypeStruct((piece, NORMAL_ROWS), jnp.bfloat16),
            jax.ShapeDtypeStruct((piece, LENGTH_ROWS), jnp.bfloat16),
            jax.ShapeDtypeStruct((piece // LANES, LANES), jnp.float32),
            jax.ShapeDtypeStruct((8, LANES), jnp.float32),
        ),
        in_specs=[VMEM, VMEM, SMEM],
        out_specs=(VMEM, VMEM, VMEM, VMEM),
        name="prepare_panels",
    )(points, normals, freestream)


def induce_kernel(
    nodes_ref, normal_side_ref, length_side_ref, onset_ref, middle_ref, right_ref, copies_ref,
    normal_ref, length_ref, inner_ref, normal_bf_ref, length_bf_ref, inner_bf_ref, total_ref,
):
    rows = nodes_ref.shape[0] * nodes_ref.shape[2]
    groups = rows // LANES
    x, y, z, circulation, tag = [nodes_ref[:, q].reshape(rows, LANES) for q in range(5)]
    piece_rows = right_ref.shape[0]
    lane = lax.broadcasted_iota(jnp.int32, (rows, LANES), 1)
    row = lax.broadcasted_iota(jnp.int32, (rows, LANES), 0)
    turned = pltpu.roll(tag, LANES - 1, 1)
    next_tag = jnp.where(lane == LANES - 1, pltpu.roll(turned, rows - 1, 0), turned)
    linked = (tag == next_tag) & ((lane < LANES - 1) | (row < rows - 1))
    strength = jnp.where(linked, circulation * (1.0 / FOUR_PI), 0.0)
    runs = [
        [(value - middle_ref[q : q + 1, :])[g * LANES : (g + 1) * LANES].T for q, value in enumerate((x, y, z))]
        for g in range(groups)
    ]
    total_ref[...] = jnp.zeros_like(total_ref)
    last = lax.broadcasted_iota(jnp.int32, (1, LANES), 1) == LANES - 1
    ones = jnp.ones((HALF, LANES), jnp.float32)
    zeros = jnp.zeros((HALF, LANES), jnp.float32)

    def put(ref, size, offset, k, value):
        for half in range(2):
            ref[half, pl.ds(offset * size + k, HALF, stride=size), :] = value[half * HALF : (half + 1) * HALF]

    for k in range(36, NORMAL_ROWS):
        for half in range(2):
            normal_ref[half, pl.ds(k, HALF, stride=NORMAL_ROWS), :] = zeros
    for half in range(2):
        for k in range(24, LENGTH_ROWS):
            inner_ref[half, pl.ds(k, HALF, stride=LENGTH_ROWS), :] = zeros
            length_ref[half, pl.ds(k, HALF + 8, stride=LENGTH_ROWS), :] = jnp.zeros((HALF + 8, LANES), jnp.float32)
        for k in range(18, 21):
            inner_ref[half, pl.ds(k, HALF, stride=LENGTH_ROWS), :] = ones
            length_ref[half, pl.ds(k, HALF + 8, stride=LENGTH_ROWS), :] = jnp.ones((HALF + 8, LANES), jnp.float32)

    for group in range(groups):
        a = runs[group]
        b = []
        for q in range(3):
            end = jnp.where(
                last, runs[(group + 1) % groups][q][0:1, 0:1], pltpu.roll(a[q][0:1, :], LANES - 1, 1)
            )
            b.append(jnp.concatenate([a[q][1:], end], axis=0))
        g = strength[group * LANES : (group + 1) * LANES].T
        ends = [g * (a[q] - b[q]) for q in range(3)]
        ends += [
            g * (a[1] * b[2] - a[2] * b[1]),
            g * (a[2] * b[0] - a[0] * b[2]),
            g * (a[0] * b[1] - a[1] * b[0]),
        ]
        for k in range(6):
            pieces = three_pieces(ends[k])
            for p in range(6):
                put(normal_ref, NORMAL_ROWS, 0, p * 6 + k, pieces[PIECE_OF_SEGMENT[p]])
        for k in range(3):
            pieces = three_pieces(-(a[k] + b[k]))
            for p in range(6):
                put(inner_ref, LENGTH_ROWS, 0, p * 3 + k, pieces[PIECE_OF_SEGMENT[p]])
            pieces = three_pieces(-2.0 * b[k])
            first = three_pieces(-2.0 * a[k])
            for p in range(6):
                put(length_ref, LENGTH_ROWS, 1, p * 3 + k, pieces[PIECE_OF_SEGMENT[p]])
                for half in range(2):
                    length_ref[half, p * 3 + k : p * 3 + k + 1, :] = first[PIECE_OF_SEGMENT[p]][half * HALF : half * HALF + 1]
        pieces = three_pieces(a[0] * b[0] + a[1] * b[1] + a[2] * b[2])
        for k in range(3):
            put(inner_ref, LENGTH_ROWS, 0, 21 + k, pieces[k])
        pieces = three_pieces(b[0] * b[0] + b[1] * b[1] + b[2] * b[2])
        first = three_pieces(a[0] * a[0] + a[1] * a[1] + a[2] * a[2])
        for k in range(3):
            put(length_ref, LENGTH_ROWS, 1, 21 + k, pieces[k])
            for half in range(2):
                length_ref[half, 21 + k : 22 + k, :] = first[k][half * HALF : half * HALF + 1]

        def narrow(i, carry):
            for source, target, size in (
                (normal_ref, normal_bf_ref, NORMAL_ROWS),
                (length_ref, length_bf_ref, LENGTH_ROWS),
                (inner_ref, inner_bf_ref, LENGTH_ROWS),
            ):
                part = pl.ds(pl.multiple_of(i * size, size), size)
                for half in range(2):
                    target[part, half * LANES : (half + 1) * LANES] = source[half, part, :].astype(jnp.bfloat16)
            return carry

        lax.fori_loop(0, HALF, narrow, 0, unroll=8)
        part = pl.ds(HALF * LENGTH_ROWS, LENGTH_ROWS)
        for half in range(2):
            length_bf_ref[part, half * LANES : (half + 1) * LANES] = length_ref[half, part, :].astype(jnp.bfloat16)

        def panel_step(b, carry):
            part = pl.ds(pl.multiple_of(b * PANEL_STEP, PANEL_STEP), PANEL_STEP)
            normal_side = normal_side_ref[part, :]
            length_side = length_side_ref[part, :]

            def form(side, ref, size, i, k):
                weights = ref[pl.ds(pl.multiple_of(i * size, size) + k * size, size), :]
                return jnp.dot(side, weights, preferred_element_type=jnp.float32)

            def length_of(square):
                square = jnp.maximum(square, 1e-30)
                return square * lax.rsqrt(square)

            def node_step(block, state):
                length, total = state
                first = block * NODE_STEP
                for k in range(NODE_STEP):
                    normal_part = form(normal_side, normal_bf_ref, NORMAL_ROWS, first, k)
                    inner = form(length_side, inner_bf_ref, LENGTH_ROWS, first, k)
                    after = length_of(form(length_side, length_bf_ref, LENGTH_ROWS, first, k + 1))
                    product = length * after
                    below = product * (product + inner) + CORE_SQ
                    total = total + ((length + after) * normal_part) * pl.reciprocal(below)
                    length = after
                return length, total

            start = (
                length_of(form(length_side, length_bf_ref, LENGTH_ROWS, 0, 0)),
                jnp.zeros((PANEL_STEP, WIDE), jnp.float32),
            )
            _, total = lax.fori_loop(0, HALF // NODE_STEP, node_step, start)
            total_ref[part, :] += total[:, :LANES] + total[:, LANES:]
            return carry

        lax.fori_loop(0, piece_rows * LANES // PANEL_STEP, panel_step, 0)

    for r in range(piece_rows):
        induced = jnp.sum(total_ref[r * LANES : (r + 1) * LANES, :].T, axis=0, keepdims=True)
        right_ref[r : r + 1, :] = -(onset_ref[r : r + 1, :] + induced)
    right = right_ref[...]
    for k in range(copies_ref.shape[0]):
        copies_ref[k] = right


def induce(nodes, panels, copies):
    piece = panels[0].shape[0]
    piece_rows = piece // LANES
    pairs = piece * nodes.size // 5
    return pl.pallas_call(
        induce_kernel,
        out_shape=(
            jax.ShapeDtypeStruct((piece_rows, LANES), jnp.float32),
            jax.ShapeDtypeStruct((copies, piece_rows, LANES), jnp.float32),
        ),
        in_specs=[VMEM] * 5,
        out_specs=(VMEM, VMEM),
        scratch_shapes=[
            pltpu.VMEM((2, HALF * NORMAL_ROWS, LANES), jnp.float32),
            pltpu.VMEM((2, (HALF + 8) * LENGTH_ROWS, LANES), jnp.float32),
            pltpu.VMEM((2, HALF * LENGTH_ROWS, LANES), jnp.float32),
            pltpu.VMEM((HALF * NORMAL_ROWS, WIDE), jnp.bfloat16),
            pltpu.VMEM(((HALF + 1) * LENGTH_ROWS, WIDE), jnp.bfloat16),
            pltpu.VMEM((HALF * LENGTH_ROWS, WIDE), jnp.bfloat16),
            pltpu.VMEM((piece, LANES), jnp.float32),
        ],
        compiler_params=pltpu.CompilerParams(vmem_limit_bytes=24 * 2**20),
        cost_estimate=pl.CostEstimate(flops=30 * pairs, bytes_accessed=2**21, transcendentals=2 * pairs),
        name="induce",
    )(nodes, *panels)


def whole_sum(value):
    return jnp.sum(value, keepdims=True)


def orthogonalize(image_ref, known_refs, column_ref):
    image = image_ref[...].reshape(-1, LANES)
    known = [ref[...] for ref in known_refs]
    coeffs = [whole_sum(image * member) for member in known]
    for coeff, member in zip(coeffs, known):
        image = image - coeff * member
    norm = jnp.sqrt(whole_sum(image * image))
    for i, value in enumerate(coeffs + [norm]):
        column_ref[i : i + 1, :] = jnp.broadcast_to(value, (1, LANES))
    return image / norm


def deal_kernel(place_ref, index_ref, near_ref, left_ref, *out_refs):
    n_col = len(out_refs) + 1
    rank, width = left_ref.shape
    piece_rows = width // LANES // n_col
    lane = lax.broadcasted_iota(jnp.int32, (8, LANES), 1)
    for shift in range(1, n_col):
        out_ref = out_refs[shift - 1]
        first = lax.rem(place_ref[1] + shift, n_col) * piece_rows
        index = jnp.zeros((8, LANES), jnp.float32)
        for r in range(piece_rows):
            base = r * (LANES + rank)
            out_ref[base : base + LANES, :] = near_ref[first + r]
            columns = pl.ds(pl.multiple_of((first + r) * LANES, LANES), LANES)
            out_ref[base + LANES : base + LANES + rank, :] = left_ref[:, columns]
            index = jnp.where(lane == r, index_ref[first + r].astype(jnp.float32), index)
        out_ref[piece_rows * (LANES + rank) :, :] = index


def deal(place, index, near, left, n_col):
    rank, width = left.shape
    piece_rows = width // LANES // n_col
    shape = jax.ShapeDtypeStruct((piece_rows * (LANES + rank) + 8, LANES), jnp.float32)
    return pl.pallas_call(
        deal_kernel,
        out_shape=(shape,) * (n_col - 1),
        in_specs=[SMEM, SMEM, VMEM, VMEM],
        out_specs=(VMEM,) * (n_col - 1),
        compiler_params=pltpu.CompilerParams(vmem_limit_bytes=16 * 2**20),
        name="deal",
    )(place, index, near, left)


def step_kernel(known_count, n_col, *refs):
    place_ref, index_refs, refs = refs[0], refs[1 : 1 + n_col], refs[1 + n_col :]
    image_ref, known_refs, refs = refs[0], refs[1 : 1 + known_count], refs[1 + known_count :]
    self_ref, near_ref, left_ref, refs = refs[0], refs[1], refs[2], refs[3:]
    dealt_refs, right_refs = refs[: n_col - 1], refs[n_col - 1 : 2 * n_col - 1]
    vector_ref, column_ref, copies_ref = refs[2 * n_col - 1 :]
    piece_rows = self_ref.shape[0]
    piece = piece_rows * LANES
    rank = right_refs[0].shape[0]
    n_wake = right_refs[0].shape[1] // piece
    vector_ref[...] = orthogonalize(image_ref, known_refs, column_ref)
    place, mine = place_ref[0], place_ref[1]

    far = [jnp.zeros((rank, LANES), jnp.float32) for _ in range(piece_rows)]
    near = [jnp.zeros((LANES, LANES), jnp.float32) for _ in range(piece_rows)]
    for shift in range(n_col):
        group = lax.rem(mine - shift + n_col, n_col)

        def chunk(w, total):
            first = (w * n_col + group) * piece_rows
            for r in range(piece_rows):
                entries = vector_ref[pl.ds(first + r, 1), :]
                columns = pl.ds(pl.multiple_of(w * piece, LANES) + r * LANES, LANES)
                total = total + right_refs[shift][:, columns] * entries
            return total

        coeff = lax.fori_loop(0, n_wake, chunk, jnp.zeros((rank, LANES), jnp.float32), unroll=4)
        coeff = jnp.sum(coeff, axis=1, keepdims=True)
        for r in range(piece_rows):
            if shift == 0:
                row_block = mine * piece_rows + r
                block = index_refs[0][row_block]
                left = left_ref[:, pl.ds(pl.multiple_of(row_block * LANES, LANES), LANES)]
                matrix = near_ref[row_block]
            else:
                base = r * (LANES + rank)
                block = index_refs[shift][r]
                left = dealt_refs[shift - 1][base + LANES : base + LANES + rank, :]
                matrix = dealt_refs[shift - 1][base : base + LANES, :]
            where = (lax.div(block, piece_rows) * n_col + group) * piece_rows + lax.rem(block, piece_rows)
            far[r] = far[r] + left * coeff
            near[r] = near[r] + matrix * vector_ref[pl.ds(where, 1), :]
    image = jnp.concatenate(
        [
            jnp.sum(near[r].T, axis=0, keepdims=True) + jnp.sum(far[r], axis=0, keepdims=True)
            for r in range(piece_rows)
        ],
        axis=0,
    )
    own = vector_ref[pl.ds(pl.multiple_of(place * piece_rows, piece_rows), piece_rows), :]
    image = self_ref[...] * own + image
    for k in range(copies_ref.shape[0]):
        copies_ref[k] = image


def arnoldi_step(place, indices, image, known, self_term, near, left, dealt, rights):
    copies, piece_rows, _ = image.shape
    total_rows = copies * piece_rows
    operands = [image, *known, self_term, near, left, *dealt, *rights]
    return pl.pallas_call(
        functools.partial(step_kernel, len(known), len(rights)),
        out_shape=(
            jax.ShapeDtypeStruct((total_rows, LANES), jnp.float32),
            jax.ShapeDtypeStruct((8, LANES), jnp.float32),
            jax.ShapeDtypeStruct((copies, piece_rows, LANES), jnp.float32),
        ),
        in_specs=[SMEM] * (1 + len(indices)) + [VMEM] * len(operands),
        out_specs=(VMEM, VMEM, VMEM),
        compiler_params=pltpu.CompilerParams(vmem_limit_bytes=24 * 2**20),
        name="arnoldi_step",
    )(place, *indices, *operands)


def small_solve(gram_matrix, projected):
    size_now = len(projected)
    factor = [[None for inner_pos in range(size_now)] for outer_pos in range(size_now)]
    for outer_pos in range(size_now):
        for inner_pos in range(outer_pos + 1):
            partial_sum = gram_matrix[outer_pos][inner_pos]
            for middle in range(inner_pos):
                partial_sum = partial_sum - factor[outer_pos][middle] * factor[inner_pos][middle]
            if inner_pos == outer_pos:
                factor[outer_pos][inner_pos] = jnp.sqrt(partial_sum)
            else:
                factor[outer_pos][inner_pos] = partial_sum / factor[inner_pos][inner_pos]
    forward = []
    for outer_pos in range(size_now):
        partial_sum = projected[outer_pos]
        for middle in range(outer_pos):
            partial_sum = partial_sum - factor[outer_pos][middle] * forward[middle]
        forward.append(partial_sum / factor[outer_pos][outer_pos])
    backward = [None for outer_pos in range(size_now)]
    for outer_pos in reversed(range(size_now)):
        partial_sum = forward[outer_pos]
        for middle in range(outer_pos + 1, size_now):
            partial_sum = partial_sum - factor[middle][outer_pos] * backward[middle]
        backward[outer_pos] = partial_sum / factor[outer_pos][outer_pos]
    return backward


def finish_kernel(place_ref, image_ref, *refs):
    known_refs, column_refs, out_ref, last_ref = refs[:KRYLOV], refs[KRYLOV : 2 * KRYLOV], refs[-2], refs[-1]
    orthogonalize(image_ref, known_refs, last_ref)
    norm = column_refs[0][0:1, :]
    columns = []
    for column, ref in enumerate(list(column_refs[1:]) + [last_ref]):
        columns.append([ref[i : i + 1, :] for i in range(column + 2)])
    gram = [
        [sum(columns[i][k] * columns[j][k] for k in range(j + 2)) for j in range(i + 1)]
        for i in range(KRYLOV)
    ]
    combination = small_solve(gram, [norm * columns[j][0] for j in range(KRYLOV)])
    piece_rows = out_ref.shape[0]
    part = pl.ds(pl.multiple_of(place_ref[0] * piece_rows, piece_rows), piece_rows)
    strengths = combination[0] * known_refs[0][part, :]
    for position in range(1, KRYLOV):
        strengths = strengths + combination[position] * known_refs[position][part, :]
    out_ref[...] = strengths


def finish(place, image, known, columns):
    piece_rows = image.shape[1]
    return pl.pallas_call(
        finish_kernel,
        out_shape=jax.ShapeDtypeStruct((piece_rows, LANES), jnp.float32),
        in_specs=[SMEM] + [VMEM] * (1 + len(known) + len(columns)),
        out_specs=VMEM,
        scratch_shapes=[pltpu.VMEM((8, LANES), jnp.float32)],
        compiler_params=pltpu.CompilerParams(vmem_limit_bytes=16 * 2**20),
        name="finish",
    )(place, image, *known, *columns)


def body(
    points,
    normals,
    freestream,
    wake_nodes,
    circulation,
    filament,
    self_term,
    near_blocks,
    near_index,
    far_left,
    far_right,
):
    everyone = ("wake", "col")
    n_wake, n_col = lax.axis_size("wake"), lax.axis_size("col")
    copies = n_wake * n_col
    piece = points.shape[1]
    piece_rows = piece // LANES
    mine = lax.axis_index("col")
    place = jnp.stack([lax.axis_index("wake") * n_col + mine, mine])

    near, index, left, right = near_blocks[:, 0, 0], near_index[:, 0, 0], far_left[0], far_right[0]
    dealt, indices, rights = [], [index], [right]
    for shift, part in enumerate(deal(place, index, near, left, n_col), 1):
        pairs = [(source, (source + shift) % n_col) for source in range(n_col)]
        dealt.append(lax.ppermute(part, "col", pairs))
        indices.append(dealt[-1][-8, :piece_rows].astype(jnp.int32))
        rights.append(lax.ppermute(right, "col", pairs))

    packed = pack_nodes(wake_nodes, circulation, filament, n_wake)
    panels = prepare_panels(points, normals, freestream)
    nodes = lax.all_to_all(packed, "wake", 0, 0, tiled=True)
    right_side, image_copies = induce(nodes, panels, copies)
    own_self = self_term.reshape(piece_rows, LANES)
    known, columns = [], []
    for _ in range(KRYLOV):
        image = lax.all_to_all(image_copies, everyone, 0, 0, tiled=True)
        vector, column, image_copies = arnoldi_step(
            place, indices, image, known, own_self, near, left, dealt, rights
        )
        known.append(vector)
        columns.append(column)
    image = lax.all_to_all(image_copies, everyone, 0, 0, tiled=True)
    strengths = finish(place, image, known, columns)
    return right_side.reshape(piece), strengths.reshape(piece)


def solution(mesh):
    in_specs = (
        P(None, ("wake", "col")),
        P(None, ("wake", "col")),
        P(),
        P(None, "wake"),
        P("wake"),
        P("wake"),
        P(("wake", "col")),
        P("wake", "col", None, None, None),
        P("wake", "col", None),
        P("col", None, "wake"),
        P("wake", None, "col"),
    )
    out_specs = (P(("wake", "col")), P(("wake", "col")))
    return jax.shard_map(body, mesh=mesh, in_specs=in_specs, out_specs=out_specs, check_vma=False)
```

time: 190 us -> 165 us (0.87)
  Pallas kernels: 91.5 us -> 68.3 us
  local copies, waits for them, and re-layouts: 2.58 us -> 8.47 us
  starting transfers between devices: 14.8 us -> 12 us
  blocking collectives: 64.6 us -> 62 us
    pallas_call x1, Pallas kernels: 70.1 us -> 43.3 us  [induce(): pl.pallas_call(induce_kernel, out_shape=(jax.ShapeDtypeStruct((piece_rows...]
    unnamed x16 -> x30, local copies, waits for them, and re-layouts: 0.03 us -> 8.47 us
    all_to_all x1, waiting for transfers between devices: 0.48 us -> 7.95 us  [body(): image = lax.all_to_all(image_copies, everyone, 0, 0, tiled=True)]
    ppermute x4 -> x2, waiting for transfers between devices: 4.66 us -> 0.01 us  [the longest x1 0.01 us: body(): rights.append(lax.ppermute(right, 'col', pairs))]
    all_to_all x1, waiting for transfers between devices: 8.71 us -> 4.23 us  [body(): nodes = lax.all_to_all(packed, 'wake', 0, 0, tiled=True)]
    pallas_call x6 -> x8, Pallas kernels: 18.3 us -> 21.9 us  [the longest x6 18.5 us: arnoldi_step(): pl.pallas_call(functools.partial(step_kernel, len(known), len(rights)), o...]
    all_to_all x6, blocking collectives: 64.6 us -> 62 us  [body(): image = lax.all_to_all(image_copies, everyone, 0, 0, tiled=True)]
    dynamic_slice x2 -> x0, local copies, waits for them, and re-layouts: 2.54 us -> none  [the longest x1 1.88 us: body(): lax.dynamic_slice_in_dim(near_own, target * piece_rows, piece_rows, 0)]
  transfers between devices with their start and end apart: 6 -> 4, of which waited for: 3 -> 2; matrix products, arithmetic and copies ran while one was open for 2% -> 0% of each run, Pallas kernels for 38% -> 29%
where the time goes in v2:
time: 165 us
  Pallas kernels  68.3 us (41%)
  blocking collectives  62 us (38%)
  waiting for transfers between devices  12.2 us (7%)
  starting transfers between devices  12 us (7%)
  local copies, waits for them, and re-layouts  8.47 us (5%)
    all_to_all x6, blocking collectives, body(): image = lax.all_to_all(image_copies, everyone, 0, 0, tiled=True)  62 us
    pallas_call x1, Pallas kernels, induce(): pl.pallas_call(induce_kernel, out_shape=(jax.ShapeDtypeStruct((piece_rows...  43.3 us
    pallas_call x6, Pallas kernels, arnoldi_step(): pl.pallas_call(functools.partial(step_kernel, len(known), len(rights)), o...  18.5 us
    unnamed x30, local copies, waits for them, and re-layouts  8.47 us
    all_to_all x1, waiting for transfers between devices, body(): image = lax.all_to_all(image_copies, everyone, 0, 0, tiled=True)  7.95 us
    all_to_all x1, starting transfers between devices, body(): nodes = lax.all_to_all(packed, 'wake', 0, 0, tiled=True)  5.94 us
    all_to_all x1, waiting for transfers between devices, body(): nodes = lax.all_to_all(packed, 'wake', 0, 0, tiled=True)  4.23 us
  transfers between devices with their start and end apart: 4, of which 2 were waited for; matrix products, arithmetic and copies ran while one was open for 0% of the time, Pallas kernels for 29%

profile of v2, /device:TPU:0, one launch (start us, length us, event | category | flops | bytes accessed | tf_op | source)
XLA Modules:
  0.0 164.5 jit_solution(2713531802516114317)
XLA Ops:
  0.6 3.0 %collective-permute-start.1 = (f32[32,16384]{1,0:T(8,128)}, f32[32,16384]{1,0:T(8,128)}, u32[]{:S(2)}, u32[]{:S(2)}) collective-permute-start(f32[32,16384]{1,0:T(8,128)} %bitcast.13), channel_id=1, source_target_pairs={{0,1},{1,0},{2,3},{3,2},{4,5},{5,4},{6,7},{7,6},{8,9},{9,8},{10,11... | collective-permute-start | bytes 6291464 | tf_op jit(solution)/shard_map/ppermute | solution.py:483
  3.6 1.5 pack_nodes.1
  5.1 5.9 %all-to-all-start = ((f32[16,5,8,128]{3,2,1,0:T(8,128)}), f32[16,5,8,128]{3,2,1,0:T(8,128)S(1)}, u32[]{:S(2)}, u32[]{:S(2)}) async-start(f32[16,5,8,128]{3,2,1,0:T(8,128)} %pack_nodes.1), calls=%async_computation | async-start | bytes 655360 | tf_op jit(solution)/shard_map/all_to_all | solution.py:487
  11.1 0.1 pad_add_fusion.place_ref.refs_0_
  11.2 0.0 copy-start.1
  11.2 1.2 copy-done.1
  12.4 0.0 copy-start.3
  12.4 0.9 copy-done.3
  13.3 0.0 copy-start.9
  13.3 0.7 copy-done.9
  14.0 1.4 deal.1
  15.4 0.5 collective-permute-start
  16.0 2.0 %prepare_panels.1 = (bf16[1024,48]{1,0:T(8,128)(2,1)}, bf16[1024,32]{1,0:T(8,128)(2,1)}, f32[8,128]{1,0:T(8,128)}, f32[8,128]{1,0:T(8,128)}) custom-call(f32[3,1024]{1,0:T(4,128)} %points_ref.1, f32[3,1024]{1,0:T(4,128)} %normals_ref.1, f32[3]{0:T(128)} %stream_ref.1), custom_call_target="tpu_custom_call" | custom-call | tf_op jit(solution)/shard_map/prepare_panels/pallas_call | solution.py:97
  17.9 4.2 %all-to-all-done.nodes_ref = f32[16,5,8,128]{3,2,1,0:T(8,128)S(1)} async-done(((f32[16,5,8,128]{3,2,1,0:T(8,128)}), f32[16,5,8,128]{3,2,1,0:T(8,128)S(1)}, u32[]{:S(2)}, u32[]{:S(2)}) %all-to-all-start) | async-done | bytes 327712 | tf_op jit(solution)/shard_map/all_to_all | solution.py:487
  22.2 0.0 copy-start.5
  22.2 0.7 copy-done.5
  22.9 0.0 copy-start.6
  22.9 1.0 copy-done.6
  23.9 0.9 copy-done.11
  24.8 0.9 copy-done.12
  25.8 0.7 copy-done.13
  26.5 0.7 copy-done.14
  27.2 0.0 copy-start.10
  27.2 43.3 %induce.1 = (f32[8,128]{1,0:T(8,128)}, f32[32,8,128]{2,1,0:T(8,128)S(1)}) custom-call(f32[16,5,8,128]{3,2,1,0:T(8,128)S(1)} %copy-done.6, bf16[1024,48]{1,0:T(8,128)(2,1)S(1)} %copy-done.11, bf16[1024,32]{1,0:T(8,128)(2,1)S(1)} %copy-done.12, f32[8,128]{1,0:T(8,128)S(1)} %copy-done.13, f32[8,128]{1,0:T(8,128)S(1)} %copy-done.14), custom_call_target="tpu_custom_call" | custom-call | flops 503316480 | bytes 2097152 | tf_op jit(solution)/shard_map/induce/pallas_call | solution.py:252
  70.5 0.6 copy-done.8
  71.2 2.6 %all-to-all-start.1 = ((f32[32,8,128]{2,1,0:T(8,128)}), f32[32,8,128]{2,1,0:T(8,128)S(1)}, u32[]{:S(2)}, u32[]{:S(2)}) async-start(f32[32,8,128]{2,1,0:T(8,128)} %copy-done.8), calls=%async_computation.1 | async-start | bytes 262144 | tf_op jit(solution)/shard_map/all_to_all | solution.py:492
  73.7 0.0 collective-permute-done.refs_7_.refs_8_.refs_9_.refs_10_.refs_11_.refs_12_
  73.7 0.7 fusion.refs_2_
  74.4 7.9 %all-to-all-done.1.refs_3_ = f32[32,8,128]{2,1,0:T(8,128)S(1)} async-done(((f32[32,8,128]{2,1,0:T(8,128)}), f32[32,8,128]{2,1,0:T(8,128)S(1)}, u32[]{:S(2)}, u32[]{:S(2)}) %all-to-all-start.1) | async-done | bytes 131104 | tf_op jit(solution)/shard_map/all_to_all | solution.py:492
  82.3 0.0 collective-permute-done.1.refs_9_.refs_10_.refs_11_.refs_12_.refs_13_.refs_14_
  82.4 0.0 copy-done
  82.4 0.0 copy-done.2
  82.4 0.0 copy-done.4
  82.4 0.0 copy-done.7
  82.4 0.0 copy-done.10
  82.4 2.9 %arnoldi_step.6 = (f32[256,128]{1,0:T(8,128)S(1)}, f32[8,128]{1,0:T(8,128)S(1)}, f32[32,8,128]{2,1,0:T(8,128)S(1)}) custom-call(s32[2]{0:T(128)S(1)} %pad_add_fusion.place_ref.refs_0_, s32[16]{0:T(128)S(1)} %bitcast.41, s32[8]{0:T(128)S(1)} %fusion.refs_2_, f32[32,8,128]{2,1,0:T(8,128)S(1)} %all-to-all-done.1.refs_3_, f32[8,128]{1,0:T(8,128)S(1)} %bitcast.34, ...), custom_call_target="tpu_custom_call" | custom-call | tf_op jit(solution)/shard_map/arnoldi_step/pallas_call | solution.py:382
  85.3 10.3 %all_to_all.40.refs_3_ = f32[32,8,128]{2,1,0:T(8,128)S(1)} all-to-all(f32[32,8,128]{2,1,0:T(8,128)S(1)} %get-tuple-element.32), channel_id=1, replica_groups=mesh['wake'=16,'col'=2] {'wake','col'}, dimensions={0} | all-to-all | bytes 262144 | tf_op jit(solution)/shard_map/all_to_all | solution.py:492
  95.7 3.1 %arnoldi_step.7 = (f32[256,128]{1,0:T(8,128)S(1)}, f32[8,128]{1,0:T(8,128)S(1)}, f32[32,8,128]{2,1,0:T(8,128)S(1)}) custom-call(s32[2]{0:T(128)S(1)} %pad_add_fusion.place_ref.refs_0_, s32[16]{0:T(128)S(1)} %bitcast.42, s32[8]{0:T(128)S(1)} %fusion.refs_2_, f32[32,8,128]{2,1,0:T(8,128)S(1)} %all_to_all.40.refs_3_, ...), custom_call_target="tpu_custom_call" | custom-call | tf_op jit(solution)/shard_map/arnoldi_step/pallas_call | solution.py:382
  98.7 10.3 %all_to_all.41.refs_3_ = f32[32,8,128]{2,1,0:T(8,128)S(1)} all-to-all(f32[32,8,128]{2,1,0:T(8,128)S(1)} %get-tuple-element.34), channel_id=1, replica_groups=mesh['wake'=16,'col'=2] {'wake','col'}, dimensions={0} | all-to-all | bytes 262144 | tf_op jit(solution)/shard_map/all_to_all | solution.py:492
  109.1 3.1 %arnoldi_step.8 = (f32[256,128]{1,0:T(8,128)S(1)}, f32[8,128]{1,0:T(8,128)S(1)}, f32[32,8,128]{2,1,0:T(8,128)S(1)}) custom-call(s32[2]{0:T(128)S(1)} %pad_add_fusion.place_ref.refs_0_, s32[16]{0:T(128)S(1)} %bitcast.43, s32[8]{0:T(128)S(1)} %fusion.refs_2_, f32[32,8,128]{2,1,0:T(8,128)S(1)} %all_to_all.41.refs_3_, ...), custom_call_target="tpu_custom_call" | custom-call | tf_op jit(solution)/shard_map/arnoldi_step/pallas_call | solution.py:382
  112.2 10.3 %all_to_all.42.refs_3_ = f32[32,8,128]{2,1,0:T(8,128)S(1)} all-to-all(f32[32,8,128]{2,1,0:T(8,128)S(1)} %get-tuple-element.36), channel_id=1, replica_groups=mesh['wake'=16,'col'=2] {'wake','col'}, dimensions={0} | all-to-all | bytes 262144 | tf_op jit(solution)/shard_map/all_to_all | solution.py:492
  122.5 3.1 %arnoldi_step.9 = (f32[256,128]{1,0:T(8,128)S(1)}, f32[8,128]{1,0:T(8,128)S(1)}, f32[32,8,128]{2,1,0:T(8,128)S(1)}) custom-call(s32[2]{0:T(128)S(1)} %pad_add_fusion.place_ref.refs_0_, s32[16]{0:T(128)S(1)} %bitcast.44, s32[8]{0:T(128)S(1)} %fusion.refs_2_, f32[32,8,128]{2,1,0:T(8,128)S(1)} %all_to_all.42.refs_3_, ...), custom_call_target="tpu_custom_call" | custom-call | tf_op jit(solution)/shard_map/arnoldi_step/pallas_call | solution.py:382
  125.6 10.3 %all_to_all.43.refs_3_ = f32[32,8,128]{2,1,0:T(8,128)S(1)} all-to-all(f32[32,8,128]{2,1,0:T(8,128)S(1)} %get-tuple-element.38), channel_id=1, replica_groups=mesh['wake'=16,'col'=2] {'wake','col'}, dimensions={0} | all-to-all | bytes 262144 | tf_op jit(solution)/shard_map/all_to_all | solution.py:492
  135.9 3.1 %arnoldi_step.10 = (f32[256,128]{1,0:T(8,128)S(1)}, f32[8,128]{1,0:T(8,128)S(1)}, f32[32,8,128]{2,1,0:T(8,128)S(1)}) custom-call(s32[2]{0:T(128)S(1)} %pad_add_fusion.place_ref.refs_0_, s32[16]{0:T(128)S(1)} %bitcast.45, s32[8]{0:T(128)S(1)} %fusion.refs_2_, f32[32,8,128]{2,1,0:T(8,128)S(1)} %all_to_all.43.refs_3_, ...), custom_call_target="tpu_custom_call" | custom-call | tf_op jit(solution)/shard_map/arnoldi_step/pallas_call | solution.py:382
  139.1 10.3 %all_to_all.44.refs_3_ = f32[32,8,128]{2,1,0:T(8,128)S(1)} all-to-all(f32[32,8,128]{2,1,0:T(8,128)S(1)} %get-tuple-element.40), channel_id=1, replica_groups=mesh['wake'=16,'col'=2] {'wake','col'}, dimensions={0} | all-to-all | bytes 262144 | tf_op jit(solution)/shard_map/all_to_all | solution.py:492
  149.4 3.2 %arnoldi_step.11 = (f32[256,128]{1,0:T(8,128)S(1)}, f32[8,128]{1,0:T(8,128)S(1)}, f32[32,8,128]{2,1,0:T(8,128)S(1)}) custom-call(s32[2]{0:T(128)S(1)} %pad_add_fusion.place_ref.refs_0_, s32[16]{0:T(128)S(1)} %bitcast.46, s32[8]{0:T(128)S(1)} %fusion.refs_2_, f32[32,8,128]{2,1,0:T(8,128)S(1)} %all_to_all.44.refs_3_, ...), custom_call_target="tpu_custom_call" | custom-call | tf_op jit(solution)/shard_map/arnoldi_step/pallas_call | solution.py:382
  152.6 10.3 %all_to_all.45.image_ref = f32[32,8,128]{2,1,0:T(8,128)S(1)} all-to-all(f32[32,8,128]{2,1,0:T(8,128)S(1)} %get-tuple-element.42), channel_id=1, replica_groups=mesh['wake'=16,'col'=2] {'wake','col'}, dimensions={0} | all-to-all | bytes 262144 | tf_op jit(solution)/shard_map/all_to_all | solution.py:498
  162.9 1.6 finish.1
  (9 shorter events, 0.0 us)
Async XLA Ops:
  0.6 81.7 %collective-permute-start.1 = (f32[32,16384]{1,0:T(8,128)}, f32[32,16384]{1,0:T(8,128)}, u32[]{:S(2)}, u32[]{:S(2)}) collective-permute-start(f32[32,16384]{1,0:T(8,128)} %bitcast.13), channel_id=1, source_target_pairs={{0,1},{1,0},{2,3},{3,2},{4,5},{5,4},{6,7},{7,6},{8,9},{9,8},{10,11... | collective-permute-start | bytes 6291464 | tf_op jit(solution)/shard_map/ppermute | solution.py:483
  5.1 17.0 %all-to-all-start = ((f32[16,5,8,128]{3,2,1,0:T(8,128)}), f32[16,5,8,128]{3,2,1,0:T(8,128)S(1)}, u32[]{:S(2)}, u32[]{:S(2)}) async-start(f32[16,5,8,128]{3,2,1,0:T(8,128)} %pack_nodes.1), calls=%async_computation | async-start | bytes 655360 | tf_op jit(solution)/shard_map/all_to_all | solution.py:487
  11.2 1.2 copy-start.1
  12.4 0.9 copy-start.3
  13.3 0.7 copy-start.9
  15.4 58.3 %collective-permute-start = (f32[1288,128]{1,0:T(8,128)}, f32[1288,128]{1,0:T(8,128)}, u32[]{:S(2)}, u32[]{:S(2)}) collective-permute-start(f32[1288,128]{1,0:T(8,128)} %deal.1), channel_id=1, source_target_pairs={{0,1},{1,0},{2,3},{3,2},{4,5},{5,4},{6,7},{7,6},{8,9},{9,8},{10,11... | collective-permute-start | bytes 1978376 | tf_op jit(solution)/shard_map/ppermute | solution.py:481
  22.2 0.7 copy-start.5
  22.9 1.0 copy-start.6
  23.9 0.9 copy-start.11
  24.8 0.9 copy-start.12
  25.8 0.7 copy-start.13
  26.5 0.7 copy-start.14
  27.2 55.2 %copy-start = (f32[1,32,16384]{2,1,0:T(8,128)S(1)}, f32[1,32,16384]{2,1,0:T(8,128)}, u32[]{:S(2)}) copy-start(f32[1,32,16384]{2,1,0:T(8,128)} %param.21) | copy-start | bytes 6291460
  27.2 55.2 %copy-start.2 = (f32[16,1,1,128,128]{4,3,2,1,0:T(8,128)S(1)}, f32[16,1,1,128,128]{4,3,2,1,0:T(8,128)}, u32[]{:S(2)}) copy-start(f32[16,1,1,128,128]{4,3,2,1,0:T(8,128)} %param.18) | copy-start | bytes 3145732
  27.2 55.2 %copy-start.4 = (f32[1,32,2048]{2,1,0:T(8,128)S(1)}, f32[1,32,2048]{2,1,0:T(8,128)}, u32[]{:S(2)}) copy-start(f32[1,32,2048]{2,1,0:T(8,128)} %param.20) | copy-start | bytes 786436
  27.2 55.2 %copy-start.7 = (f32[1024]{0:T(1024)S(1)}, f32[1024]{0:T(1024)}, u32[]{:S(2)}) copy-start(f32[1024]{0:T(1024)} %param.17) | copy-start | bytes 12292
  27.2 55.2 %copy-start.10 = (s32[16,1,1]{0,2,1:T(1,128)S(1)}, s32[16,1,1]{0,2,1:T(1,128)}, u32[]{:S(2)}) copy-start(s32[16,1,1]{0,2,1:T(1,128)} %param.19) | copy-start | bytes 196
  70.5 0.6 copy-start.8
  71.2 11.2 %all-to-all-start.1 = ((f32[32,8,128]{2,1,0:T(8,128)}), f32[32,8,128]{2,1,0:T(8,128)S(1)}, u32[]{:S(2)}, u32[]{:S(2)}) async-start(f32[32,8,128]{2,1,0:T(8,128)} %copy-done.8), calls=%async_computation.1 | async-start | bytes 262144 | tf_op jit(solution)/shard_map/all_to_all | solution.py:492

commit v3 on v2

--- a/solution.py
+++ b/solution.py
@@ -12,17 +12,20 @@
 CORE_SQ = 0.01
 FOUR_PI = 4.0 * math.pi
 LANES = 128
-PIECE_OF_PANEL = (0, 0, 1, 0, 2, 1)
-PIECE_OF_SEGMENT = (0, 1, 0, 2, 0, 1)
-NORMAL_ROWS = 48
-LENGTH_ROWS = 32
+NORMAL_PRODUCTS = ((0, 0), (0, 1), (1, 0), (0, 2), (2, 0))
+LENGTH_PRODUCTS = NORMAL_PRODUCTS + ((1, 1),)
+FEATURES = 32
+RUN = 4
+DEPTH = FEATURES * RUN
 WIDE = 2 * LANES
 HALF = LANES // 2
-PANEL_STEP = 128
-NODE_STEP = 32
+BLOCKS = HALF // RUN
+PANEL_STEP = 256
+BLOCK_STEP = 8
 
 VMEM = pl.BlockSpec(memory_space=pltpu.VMEM)
 SMEM = pl.BlockSpec(memory_space=pltpu.SMEM)
+HBM = pl.BlockSpec(memory_space=pltpu.HBM)
 
 
 def pack_kernel(nodes_ref, circulation_ref, filament_ref, out_ref):
@@ -57,8 +60,11 @@
     return high, middle, low
 
 
-def panels_kernel(points_ref, normals_ref, stream_ref, normal_side_ref, length_side_ref, onset_ref, middle_ref):
-    piece_rows = onset_ref.shape[0]
+def panels_kernel(
+    points_ref, normals_ref, stream_ref, normal_side_out, length_side_out, info_out,
+    normal_side_ref, length_side_ref, info_ref, left,
+):
+    piece_rows = info_ref.shape[0] - 8
 
     def spread(ref, q):
         return jnp.concatenate(
@@ -68,8 +74,12 @@
     points = [spread(points_ref, q) for q in range(3)]
     normals = [spread(normals_ref, q) for q in range(3)]
     middle = [0.5 * (jnp.max(p, keepdims=True) + jnp.min(p, keepdims=True)) for p in points]
+    info_ref[...] = jnp.zeros_like(info_ref)
+    info_ref[0:piece_rows, :] = (
+        stream_ref[0] * normals[0] + stream_ref[1] * normals[1] + stream_ref[2] * normals[2]
+    )
     for q in range(3):
-        middle_ref[q : q + 1, :] = jnp.broadcast_to(middle[q], (1, LANES))
+        info_ref[piece_rows + q : piece_rows + q + 1, :] = jnp.broadcast_to(middle[q], (1, LANES))
     px, py, pz = [points[q] - middle[q] for q in range(3)]
     features = [
         normals[1] * pz - normals[2] * py,
@@ -77,19 +87,37 @@
         normals[0] * py - normals[1] * px,
         normals[0], normals[1], normals[2],
     ]
+    blank = jnp.zeros_like(px)
     pieces = [three_pieces(feature) for feature in features]
-    side = [pieces[k][p] for p in PIECE_OF_PANEL for k in range(6)]
-    side += [jnp.zeros_like(px)] * (NORMAL_ROWS - len(side))
+    side = [pieces[k][p] for p, _ in NORMAL_PRODUCTS for k in range(6)]
+    side += [blank] * (FEATURES - len(side))
     pieces = [three_pieces(value) for value in (px, py, pz)]
-    side += [pieces[k][p] for p in PIECE_OF_PANEL for k in range(3)]
+    side += [pieces[k][p] for p, _ in LENGTH_PRODUCTS for k in range(3)]
     side += list(three_pieces(px * px + py * py + pz * pz)) + [jnp.ones_like(px)] * 3
-    side += [jnp.zeros_like(px)] * (LANES - len(side))
+    side += [blank] * (LANES - len(side))
+    column = lax.broadcasted_iota(jnp.int32, (FEATURES, DEPTH), 1)
+    first = lax.broadcasted_iota(jnp.int32, (FEATURES, DEPTH), 0) * RUN
+    again = jnp.where((column >= first) & (column < first + RUN), 1.0, 0.0).astype(jnp.bfloat16)
     for r in range(piece_rows):
         own = slice(r * LANES, (r + 1) * LANES)
-        turned = jnp.concatenate([value[r : r + 1, :] for value in side], axis=0).T
-        normal_side_ref[own, :] = turned[:, :NORMAL_ROWS].astype(jnp.bfloat16)
-        length_side_ref[own, :] = turned[:, NORMAL_ROWS : NORMAL_ROWS + LENGTH_ROWS].astype(jnp.bfloat16)
-    onset_ref[...] = stream_ref[0] * normals[0] + stream_ref[1] * normals[1] + stream_ref[2] * normals[2]
+        turned = jnp.concatenate([value[r : r + 1, :] for value in side], axis=0).T.astype(jnp.bfloat16)
+        for ref, start in ((normal_side_ref, 0), (length_side_ref, FEATURES)):
+            wide = jnp.dot(turned[:, start : start + FEATURES], again, preferred_element_type=jnp.float32)
+            ref[own, :] = wide.astype(jnp.bfloat16)
+    leaving = [
+        pltpu.make_async_copy(source, target, left.at[i])
+        for i, (source, target) in enumerate(
+            (
+                (normal_side_ref, normal_side_out),
+                (length_side_ref, length_side_out),
+                (info_ref, info_out),
+            )
+        )
+    ]
+    for copy in leaving:
+        copy.start()
+    for copy in leaving:
+        copy.wait()
 
 
 def prepare_panels(points, normals, freestream):
@@ -97,21 +125,42 @@
     return pl.pallas_call(
         panels_kernel,
         out_shape=(
-            jax.ShapeDtypeStruct((piece, NORMAL_ROWS), jnp.bfloat16),
-            jax.ShapeDtypeStruct((piece, LENGTH_ROWS), jnp.bfloat16),
-            jax.ShapeDtypeStruct((piece // LANES, LANES), jnp.float32),
-            jax.ShapeDtypeStruct((8, LANES), jnp.float32),
+            jax.ShapeDtypeStruct((piece, DEPTH), jnp.bfloat16),
+            jax.ShapeDtypeStruct((piece, DEPTH), jnp.bfloat16),
+            jax.ShapeDtypeStruct((piece // LANES + 8, LANES), jnp.float32),
         ),
         in_specs=[VMEM, VMEM, SMEM],
-        out_specs=(VMEM, VMEM, VMEM, VMEM),
+        out_specs=(HBM, HBM, HBM),
+        scratch_shapes=[
+            pltpu.VMEM((piece, DEPTH), jnp.bfloat16),
+            pltpu.VMEM((piece, DEPTH), jnp.bfloat16),
+            pltpu.VMEM((piece // LANES + 8, LANES), jnp.float32),
+            pltpu.SemaphoreType.DMA((3,)),
+        ],
         name="prepare_panels",
     )(points, normals, freestream)
 
 
 def induce_kernel(
-    nodes_ref, normal_side_ref, length_side_ref, onset_ref, middle_ref, right_ref, copies_ref,
-    normal_ref, length_ref, inner_ref, normal_bf_ref, length_bf_ref, inner_bf_ref, total_ref,
+    nodes_in, normal_side_in, length_side_in, info_in, right_ref, copies_ref,
+    nodes_ref, normal_side_ref, length_side_ref, info_ref,
+    normal_ref, length_ref, inner_ref, normal_pick_ref, length_pick_ref, total_ref, arrived,
 ):
+    fetches = [
+        pltpu.make_async_copy(source, target, arrived.at[i])
+        for i, (source, target) in enumerate(
+            (
+                (nodes_in, nodes_ref),
+                (info_in, info_ref),
+                (normal_side_in, normal_side_ref),
+                (length_side_in, length_side_ref),
+            )
+        )
+    ]
+    for fetch in fetches:
+        fetch.start()
+    fetches[0].wait()
+    fetches[1].wait()
     rows = nodes_ref.shape[0] * nodes_ref.shape[2]
     groups = rows // LANES
     x, y, z, circulation, tag = [nodes_ref[:, q].reshape(rows, LANES) for q in range(5)]
@@ -123,28 +172,28 @@
     linked = (tag == next_tag) & ((lane < LANES - 1) | (row < rows - 1))
     strength = jnp.where(linked, circulation * (1.0 / FOUR_PI), 0.0)
     runs = [
-        [(value - middle_ref[q : q + 1, :])[g * LANES : (g + 1) * LANES].T for q, value in enumerate((x, y, z))]
+        [
+            (value - info_ref[piece_rows + q : piece_rows + q + 1, :])[g * LANES : (g + 1) * LANES].T
+            for q, value in enumerate((x, y, z))
+        ]
         for g in range(groups)
     ]
     total_ref[...] = jnp.zeros_like(total_ref)
     last = lax.broadcasted_iota(jnp.int32, (1, LANES), 1) == LANES - 1
-    ones = jnp.ones((HALF, LANES), jnp.float32)
-    zeros = jnp.zeros((HALF, LANES), jnp.float32)
-
-    def put(ref, size, offset, k, value):
-        for half in range(2):
-            ref[half, pl.ds(offset * size + k, HALF, stride=size), :] = value[half * HALF : (half + 1) * HALF]
-
-    for k in range(36, NORMAL_ROWS):
-        for half in range(2):
-            normal_ref[half, pl.ds(k, HALF, stride=NORMAL_ROWS), :] = zeros
-    for half in range(2):
-        for k in range(24, LENGTH_ROWS):
-            inner_ref[half, pl.ds(k, HALF, stride=LENGTH_ROWS), :] = zeros
-            length_ref[half, pl.ds(k, HALF + 8, stride=LENGTH_ROWS), :] = jnp.zeros((HALF + 8, LANES), jnp.float32)
-        for k in range(18, 21):
-            inner_ref[half, pl.ds(k, HALF, stride=LENGTH_ROWS), :] = ones
-            length_ref[half, pl.ds(k, HALF + 8, stride=LENGTH_ROWS), :] = jnp.ones((HALF + 8, LANES), jnp.float32)
+    blank = jnp.zeros((LANES, LANES), jnp.float32)
+    ones = jnp.ones((LANES, LANES), jnp.float32)
+
+    def put(ref, features, blocks, to=0):
+        features = features + [blank] * (FEATURES - len(features))
+        count = 16 // RUN
+        for k in range(0, FEATURES, count):
+            for half in range(2):
+                for block in range(blocks):
+                    start = half * HALF + block * RUN
+                    rows = jnp.concatenate([value[start : start + RUN] for value in features[k : k + count]], axis=0)
+                    ref[to + block, k * RUN : (k + count) * RUN, half * LANES : (half + 1) * LANES] = rows.astype(
+                        jnp.bfloat16
+                    )
 
     for group in range(groups):
         a = runs[group]
@@ -161,77 +210,58 @@
             g * (a[2] * b[0] - a[0] * b[2]),
             g * (a[0] * b[1] - a[1] * b[0]),
         ]
-        for k in range(6):
-            pieces = three_pieces(ends[k])
-            for p in range(6):
-                put(normal_ref, NORMAL_ROWS, 0, p * 6 + k, pieces[PIECE_OF_SEGMENT[p]])
-        for k in range(3):
-            pieces = three_pieces(-(a[k] + b[k]))
-            for p in range(6):
-                put(inner_ref, LENGTH_ROWS, 0, p * 3 + k, pieces[PIECE_OF_SEGMENT[p]])
-            pieces = three_pieces(-2.0 * b[k])
-            first = three_pieces(-2.0 * a[k])
-            for p in range(6):
-                put(length_ref, LENGTH_ROWS, 1, p * 3 + k, pieces[PIECE_OF_SEGMENT[p]])
-                for half in range(2):
-                    length_ref[half, p * 3 + k : p * 3 + k + 1, :] = first[PIECE_OF_SEGMENT[p]][half * HALF : half * HALF + 1]
-        pieces = three_pieces(a[0] * b[0] + a[1] * b[1] + a[2] * b[2])
-        for k in range(3):
-            put(inner_ref, LENGTH_ROWS, 0, 21 + k, pieces[k])
-        pieces = three_pieces(b[0] * b[0] + b[1] * b[1] + b[2] * b[2])
-        first = three_pieces(a[0] * a[0] + a[1] * a[1] + a[2] * a[2])
-        for k in range(3):
-            put(length_ref, LENGTH_ROWS, 1, 21 + k, pieces[k])
-            for half in range(2):
-                length_ref[half, 21 + k : 22 + k, :] = first[k][half * HALF : half * HALF + 1]
-
-        def narrow(i, carry):
-            for source, target, size in (
-                (normal_ref, normal_bf_ref, NORMAL_ROWS),
-                (length_ref, length_bf_ref, LENGTH_ROWS),
-                (inner_ref, inner_bf_ref, LENGTH_ROWS),
-            ):
-                part = pl.ds(pl.multiple_of(i * size, size), size)
-                for half in range(2):
-                    target[part, half * LANES : (half + 1) * LANES] = source[half, part, :].astype(jnp.bfloat16)
-            return carry
-
-        lax.fori_loop(0, HALF, narrow, 0, unroll=8)
-        part = pl.ds(HALF * LENGTH_ROWS, LENGTH_ROWS)
-        for half in range(2):
-            length_bf_ref[part, half * LANES : (half + 1) * LANES] = length_ref[half, part, :].astype(jnp.bfloat16)
+        pieces = [three_pieces(value) for value in ends]
+        put(normal_ref, [pieces[k][p] for _, p in NORMAL_PRODUCTS for k in range(6)], BLOCKS)
+
+        def length_rows(linear, square):
+            pieces = [three_pieces(value) for value in linear]
+            rows = [pieces[k][p] for _, p in LENGTH_PRODUCTS for k in range(3)]
+            return rows + [ones] * 3 + list(three_pieces(square))
+
+        inner = length_rows([-(a[q] + b[q]) for q in range(3)], a[0] * b[0] + a[1] * b[1] + a[2] * b[2])
+        put(inner_ref, inner, BLOCKS)
+        after = length_rows([-2.0 * b[q] for q in range(3)], b[0] * b[0] + b[1] * b[1] + b[2] * b[2])
+        put(length_ref, after, BLOCKS)
+        start = length_rows([-2.0 * a[q] for q in range(3)], a[0] * a[0] + a[1] * a[1] + a[2] * a[2])
+        put(length_ref, start, 1, BLOCKS)
+        if group == 0:
+            fetches[2].wait()
+            fetches[3].wait()
 
         def panel_step(b, carry):
             part = pl.ds(pl.multiple_of(b * PANEL_STEP, PANEL_STEP), PANEL_STEP)
-            normal_side = normal_side_ref[part, :]
-            length_side = length_side_ref[part, :]
-
-            def form(side, ref, size, i, k):
-                weights = ref[pl.ds(pl.multiple_of(i * size, size) + k * size, size), :]
-                return jnp.dot(side, weights, preferred_element_type=jnp.float32)
+            place = lax.broadcasted_iota(jnp.int32, (1, DEPTH), 1) % RUN
+            for j in range(RUN):
+                mask = jnp.where(place == j, 1.0, 0.0).astype(jnp.bfloat16)
+                normal_pick_ref[j] = normal_side_ref[part, :] * mask
+                length_pick_ref[j] = length_side_ref[part, :] * mask
+
+            def form(pick_ref, j, weights):
+                return jnp.dot(pick_ref[j], weights, preferred_element_type=jnp.float32)
 
             def length_of(square):
                 square = jnp.maximum(square, 1e-30)
                 return square * lax.rsqrt(square)
 
-            def node_step(block, state):
+            def node_step(step, state):
                 length, total = state
-                first = block * NODE_STEP
-                for k in range(NODE_STEP):
-                    normal_part = form(normal_side, normal_bf_ref, NORMAL_ROWS, first, k)
-                    inner = form(length_side, inner_bf_ref, LENGTH_ROWS, first, k)
-                    after = length_of(form(length_side, length_bf_ref, LENGTH_ROWS, first, k + 1))
-                    product = length * after
-                    below = product * (product + inner) + CORE_SQ
-                    total = total + ((length + after) * normal_part) * pl.reciprocal(below)
-                    length = after
+                for i in range(BLOCK_STEP):
+                    block = step * BLOCK_STEP + i
+                    for j in range(RUN):
+                        normal_part = form(normal_pick_ref, j, normal_ref[block])
+                        inner = form(length_pick_ref, j, inner_ref[block])
+                        after = length_of(form(length_pick_ref, j, length_ref[block]))
+                        product = length * after
+                        below = product * (product + inner) + CORE_SQ
+                        total = total + ((length + after) * normal_part) * pl.reciprocal(below)
+                        length = after
                 return length, total
 
             start = (
-                length_of(form(length_side, length_bf_ref, LENGTH_ROWS, 0, 0)),
+                length_of(form(length_pick_ref, 0, length_ref[BLOCKS])),
                 jnp.zeros((PANEL_STEP, WIDE), jnp.float32),
             )
-            _, total = lax.fori_loop(0, HALF // NODE_STEP, node_step, start)
+            _, total = lax.fori_loop(0, BLOCKS // BLOCK_STEP, node_step, start)
             total_ref[part, :] += total[:, :LANES] + total[:, LANES:]
             return carry
 
@@ -239,7 +269,7 @@
 
     for r in range(piece_rows):
         induced = jnp.sum(total_ref[r * LANES : (r + 1) * LANES, :].T, axis=0, keepdims=True)
-        right_ref[r : r + 1, :] = -(onset_ref[r : r + 1, :] + induced)
+        right_ref[r : r + 1, :] = -(info_ref[r : r + 1, :] + induced)
     right = right_ref[...]
     for k in range(copies_ref.shape[0]):
         copies_ref[k] = right
@@ -255,18 +285,22 @@
             jax.ShapeDtypeStruct((piece_rows, LANES), jnp.float32),
             jax.ShapeDtypeStruct((copies, piece_rows, LANES), jnp.float32),
         ),
-        in_specs=[VMEM] * 5,
+        in_specs=[HBM] * 4,
         out_specs=(VMEM, VMEM),
         scratch_shapes=[
-            pltpu.VMEM((2, HALF * NORMAL_ROWS, LANES), jnp.float32),
-            pltpu.VMEM((2, (HALF + 8) * LENGTH_ROWS, LANES), jnp.float32),
-            pltpu.VMEM((2, HALF * LENGTH_ROWS, LANES), jnp.float32),
-            pltpu.VMEM((HALF * NORMAL_ROWS, WIDE), jnp.bfloat16),
-            pltpu.VMEM(((HALF + 1) * LENGTH_ROWS, WIDE), jnp.bfloat16),
-            pltpu.VMEM((HALF * LENGTH_ROWS, WIDE), jnp.bfloat16),
+            pltpu.VMEM(nodes.shape, jnp.float32),
+            pltpu.VMEM((piece, DEPTH), jnp.bfloat16),
+            pltpu.VMEM((piece, DEPTH), jnp.bfloat16),
+            pltpu.VMEM((piece_rows + 8, LANES), jnp.float32),
+            pltpu.VMEM((BLOCKS, DEPTH, WIDE), jnp.bfloat16),
+            pltpu.VMEM((BLOCKS + 1, DEPTH, WIDE), jnp.bfloat16),
+            pltpu.VMEM((BLOCKS, DEPTH, WIDE), jnp.bfloat16),
+            pltpu.VMEM((RUN, PANEL_STEP, DEPTH), jnp.bfloat16),
+            pltpu.VMEM((RUN, PANEL_STEP, DEPTH), jnp.bfloat16),
             pltpu.VMEM((piece, LANES), jnp.float32),
+            pltpu.SemaphoreType.DMA((4,)),
         ],
-        compiler_params=pltpu.CompilerParams(vmem_limit_bytes=24 * 2**20),
+        compiler_params=pltpu.CompilerParams(vmem_limit_bytes=60 * 2**20),
         cost_estimate=pl.CostEstimate(flops=30 * pairs, bytes_accessed=2**21, transcendentals=2 * pairs),
         name="induce",
     )(nodes, *panels)
@@ -320,18 +354,42 @@
     )(place, index, near, left)
 
 
-def step_kernel(known_count, n_col, *refs):
-    place_ref, index_refs, refs = refs[0], refs[1 : 1 + n_col], refs[1 + n_col :]
+def step_kernel(known_count, n_col, opening, *refs):
+    place_ref, own_index_ref, refs = refs[0], refs[1], refs[2:]
+    other = n_col - 1
+    index_refs, refs = (None, refs) if opening else (refs[:other], refs[other:])
     image_ref, known_refs, refs = refs[0], refs[1 : 1 + known_count], refs[1 + known_count :]
-    self_ref, near_ref, left_ref, refs = refs[0], refs[1], refs[2], refs[3:]
-    dealt_refs, right_refs = refs[: n_col - 1], refs[n_col - 1 : 2 * n_col - 1]
-    vector_ref, column_ref, copies_ref = refs[2 * n_col - 1 :]
+    self_ref, near_ref, left_ref, right_ref, refs = refs[0], refs[1], refs[2], refs[3], refs[4:]
+    dealt_refs, right_refs, refs = refs[:other], refs[other : 2 * other], refs[2 * other :]
+    vector_ref, column_ref, copies_ref = refs[:3]
+    fetches = []
+    if opening:
+        dealt_in, right_in = dealt_refs, right_refs
+        refs = refs[3:]
+        index_refs, dealt_refs, right_refs = refs[:other], refs[other : 2 * other], refs[2 * other : 3 * other]
+        arrived = refs[3 * other]
+        for i, (source, target) in enumerate(
+            list(zip(dealt_in, dealt_refs)) + list(zip(right_in, right_refs))
+        ):
+            fetches.append(pltpu.make_async_copy(source, target, arrived.at[i]))
+            fetches[-1].start()
     piece_rows = self_ref.shape[0]
     piece = piece_rows * LANES
-    rank = right_refs[0].shape[0]
-    n_wake = right_refs[0].shape[1] // piece
+    rank = right_ref.shape[0]
+    n_wake = right_ref.shape[1] // piece
     vector_ref[...] = orthogonalize(image_ref, known_refs, column_ref)
     place, mine = place_ref[0], place_ref[1]
+    for fetch in fetches:
+        fetch.wait()
+    if opening:
+        lane = lax.broadcasted_iota(jnp.int32, (1, LANES), 1)
+        for index_ref, dealt_ref in zip(index_refs, dealt_refs):
+            last = dealt_ref.shape[0] - 8
+            row = dealt_ref[last : last + 1, :]
+            for r in range(piece_rows):
+                index_ref[r] = jnp.sum(jnp.where(lane == r, row, 0.0)).astype(jnp.int32)
+    index_refs = (own_index_ref, *index_refs)
+    right_refs = (right_ref, *right_refs)
 
     far = [jnp.zeros((rank, LANES), jnp.float32) for _ in range(piece_rows)]
     near = [jnp.zeros((LANES, LANES), jnp.float32) for _ in range(piece_rows)]
@@ -375,22 +433,39 @@
         copies_ref[k] = image
 
 
-def arnoldi_step(place, indices, image, known, self_term, near, left, dealt, rights):
+def arnoldi_step(place, index, image, known, self_term, near, left, right, others):
     copies, piece_rows, _ = image.shape
-    total_rows = copies * piece_rows
-    operands = [image, *known, self_term, near, left, *dealt, *rights]
-    return pl.pallas_call(
-        functools.partial(step_kernel, len(known), len(rights)),
-        out_shape=(
-            jax.ShapeDtypeStruct((total_rows, LANES), jnp.float32),
-            jax.ShapeDtypeStruct((8, LANES), jnp.float32),
-            jax.ShapeDtypeStruct((copies, piece_rows, LANES), jnp.float32),
-        ),
-        in_specs=[SMEM] * (1 + len(indices)) + [VMEM] * len(operands),
-        out_specs=(VMEM, VMEM, VMEM),
+    opening = len(known) == 0
+    dealt, rights = others[-2:]
+    out_shape = [
+        jax.ShapeDtypeStruct((copies * piece_rows, LANES), jnp.float32),
+        jax.ShapeDtypeStruct((8, LANES), jnp.float32),
+        jax.ShapeDtypeStruct((copies, piece_rows, LANES), jnp.float32),
+    ]
+    out_specs, scratch = [VMEM] * 3, []
+    indices = [] if opening else others[0]
+    operands = [image, *known, self_term, near, left, right]
+    in_specs = [SMEM] * (2 + len(indices)) + [VMEM] * len(operands)
+    in_specs += [HBM if opening else VMEM] * (len(dealt) + len(rights))
+    if opening:
+        out_shape += [jax.ShapeDtypeStruct((piece_rows,), jnp.int32) for _ in dealt]
+        out_shape += [jax.ShapeDtypeStruct(value.shape, jnp.float32) for value in (*dealt, *rights)]
+        out_specs += [SMEM] * len(dealt) + [VMEM] * (len(dealt) + len(rights))
+        scratch = [pltpu.SemaphoreType.DMA((max(1, len(dealt) + len(rights)),))]
+    results = pl.pallas_call(
+        functools.partial(step_kernel, len(known), 1 + len(dealt), opening),
+        out_shape=tuple(out_shape),
+        in_specs=in_specs,
+        out_specs=tuple(out_specs),
+        scratch_shapes=scratch,
         compiler_params=pltpu.CompilerParams(vmem_limit_bytes=24 * 2**20),
         name="arnoldi_step",
-    )(place, *indices, *operands)
+    )(place, index, *indices, *operands, *dealt, *rights)
+    if opening:
+        count = len(dealt)
+        rest = results[3:]
+        others = (rest[:count], rest[count : 2 * count], rest[2 * count :])
+    return results[:3], others
 
 
 def small_solve(gram_matrix, projected):
@@ -475,12 +550,12 @@
     place = jnp.stack([lax.axis_index("wake") * n_col + mine, mine])
 
     near, index, left, right = near_blocks[:, 0, 0], near_index[:, 0, 0], far_left[0], far_right[0]
-    dealt, indices, rights = [], [index], [right]
+    dealt, rights = [], []
     for shift, part in enumerate(deal(place, index, near, left, n_col), 1):
         pairs = [(source, (source + shift) % n_col) for source in range(n_col)]
         dealt.append(lax.ppermute(part, "col", pairs))
-        indices.append(dealt[-1][-8, :piece_rows].astype(jnp.int32))
         rights.append(lax.ppermute(right, "col", pairs))
+    others = (dealt, rights)
 
     packed = pack_nodes(wake_nodes, circulation, filament, n_wake)
     panels = prepare_panels(points, normals, freestream)
@@ -490,8 +565,8 @@
     known, columns = [], []
     for _ in range(KRYLOV):
         image = lax.all_to_all(image_copies, everyone, 0, 0, tiled=True)
-        vector, column, image_copies = arnoldi_step(
-            place, indices, image, known, own_self, near, left, dealt, rights
+        (vector, column, image_copies), others = arnoldi_step(
+            place, index, image, known, own_self, near, left, right, others
         )
         known.append(vector)
         columns.append(column)

time: 165 us -> 152 us (0.921)
  Pallas kernels: 68.3 us -> 60.2 us
  local copies, waits for them, and re-layouts: 8.47 us -> 3.59 us
    pallas_call x7, Pallas kernels: 20.5 us -> 15.3 us  [the longest x6 13.1 us: arnoldi_step(): pl.pallas_call(functools.partial(step_kernel, len(known), 1 + len(dealt),...]
    unnamed x30 -> x18, local copies, waits for them, and re-layouts: 8.47 us -> 3.59 us
    pallas_call x1, Pallas kernels: 43.3 us -> 40.4 us  [induce(): pl.pallas_call(induce_kernel, out_shape=(jax.ShapeDtypeStruct((piece_rows...]
  transfers between devices with their start and end apart: 4 -> 4, of which waited for: 2 -> 2; matrix products, arithmetic and copies ran while one was open for 0% -> 0% of each run, Pallas kernels for 29% -> 30%
where the time goes in v3:
time: 152 us; the launch traced here: 151 us
  blocking collectives  62 us (41%)
  Pallas kernels  60.2 us (40%)
  waiting for transfers between devices  12.7 us (8%)
  starting transfers between devices  12.1 us (8%)
  local copies, waits for them, and re-layouts  3.59 us (2%)
    all_to_all x6, blocking collectives, body(): image = lax.all_to_all(image_copies, everyone, 0, 0, tiled=True)  62 us
    pallas_call x1, Pallas kernels, induce(): pl.pallas_call(induce_kernel, out_shape=(jax.ShapeDtypeStruct((piece_rows...  40.4 us
    pallas_call x6, Pallas kernels, arnoldi_step(): pl.pallas_call(functools.partial(step_kernel, len(known), 1 + len(dealt),...  13.1 us
    all_to_all x1, waiting for transfers between devices, body(): image = lax.all_to_all(image_copies, everyone, 0, 0, tiled=True)  8.61 us
    all_to_all x1, starting transfers between devices, body(): nodes = lax.all_to_all(packed, 'wake', 0, 0, tiled=True)  5.94 us
    all_to_all x1, waiting for transfers between devices, body(): nodes = lax.all_to_all(packed, 'wake', 0, 0, tiled=True)  4.04 us
    unnamed x18, local copies, waits for them, and re-layouts  3.59 us
  transfers between devices with their start and end apart: 4, of which 2 were waited for; matrix products, arithmetic and copies ran while one was open for 0% of the time, Pallas kernels for 30%

profile of v3, /device:TPU:0, one launch (start us, length us, event | category | flops | bytes accessed | tf_op | source)
XLA Modules:
  0.0 151.4 jit_solution(8066992015329888747)
XLA Ops:
  0.6 3.0 %collective-permute-start.1 = (f32[32,16384]{1,0:T(8,128)}, f32[32,16384]{1,0:T(8,128)}, u32[]{:S(2)}, u32[]{:S(2)}) collective-permute-start(f32[32,16384]{1,0:T(8,128)} %bitcast.11), channel_id=1, source_target_pairs={{0,1},{1,0},{2,3},{3,2},{4,5},{5,4},{6,7},{7,6},{8,9},{9,8},{10,11... | collective-permute-start | bytes 6291464 | tf_op jit(solution)/shard_map/ppermute | solution.py:557
  3.6 1.5 pack_nodes.1
  5.1 5.9 %all-to-all-start = ((f32[16,5,8,128]{3,2,1,0:T(8,128)}), f32[16,5,8,128]{3,2,1,0:T(8,128)S(1)}, u32[]{:S(2)}, u32[]{:S(2)}) async-start(f32[16,5,8,128]{3,2,1,0:T(8,128)} %pack_nodes.1), calls=%async_computation | async-start | bytes 655360 | tf_op jit(solution)/shard_map/all_to_all | solution.py:562
  11.1 0.1 pad_add_fusion.place_ref.refs_0_
  11.2 0.0 copy-start.1
  11.2 1.2 copy-done.1
  12.4 0.0 copy-start.3
  12.4 0.9 copy-done.3
  13.3 0.0 copy-start.6
  13.3 0.7 copy-done.6
  14.0 1.4 deal.1
  15.4 0.5 collective-permute-start
  16.0 2.2 %prepare_panels.1 = (bf16[1024,128]{1,0:T(8,128)(2,1)}, bf16[1024,128]{1,0:T(8,128)(2,1)}, f32[16,128]{1,0:T(8,128)}) custom-call(f32[3,1024]{1,0:T(4,128)} %points_ref.1, f32[3,1024]{1,0:T(4,128)} %normals_ref.1, f32[3]{0:T(128)} %stream_ref.1), custom_call_target="tpu_custom_call" | custom-call | tf_op jit(solution)/shard_map/prepare_panels/pallas_call | solution.py:125
  18.1 4.0 %all-to-all-done.nodes_in = f32[16,5,8,128]{3,2,1,0:T(8,128)S(1)} async-done(((f32[16,5,8,128]{3,2,1,0:T(8,128)}), f32[16,5,8,128]{3,2,1,0:T(8,128)S(1)}, u32[]{:S(2)}, u32[]{:S(2)}) %all-to-all-start) | async-done | bytes 327712 | tf_op jit(solution)/shard_map/all_to_all | solution.py:562
  22.2 0.0 copy-start.8
  22.2 0.7 copy-done.8
  22.9 0.0 copy-start
  22.9 0.0 copy-start.2
  22.9 0.0 copy-start.4
  22.9 0.0 copy-start.5
  22.9 0.0 copy-start.7
  23.0 40.4 %induce.1 = (f32[8,128]{1,0:T(8,128)}, f32[32,8,128]{2,1,0:T(8,128)}) custom-call(f32[16,5,8,128]{3,2,1,0:T(8,128)} %copy-done.8, bf16[1024,128]{1,0:T(8,128)(2,1)} %get-tuple-element.28.normal_side_in, bf16[1024,128]{1,0:T(8,128)(2,1)} %get-tuple-element.29.length_side_in, f32[16,128]{1,0:T(8,128)} %get-tuple-element.30.info_in), custom_call_target="tpu_custom_call" | custom-call | flops 503316480 | bytes 2097152 | tf_op jit(solution)/shard_map/induce/pallas_call | solution.py:282
  63.4 2.6 %all-to-all-start.1 = ((f32[32,8,128]{2,1,0:T(8,128)}), f32[32,8,128]{2,1,0:T(8,128)S(1)}, u32[]{:S(2)}, u32[]{:S(2)}) async-start(f32[32,8,128]{2,1,0:T(8,128)} %get-tuple-element.32), calls=%async_computation.1 | async-start | bytes 262144 | tf_op jit(solution)/shard_map/all_to_all | solution.py:567
  66.0 0.0 collective-permute-done.refs_7_
  66.0 8.6 %all-to-all-done.1.refs_2_ = f32[32,8,128]{2,1,0:T(8,128)S(1)} async-done(((f32[32,8,128]{2,1,0:T(8,128)}), f32[32,8,128]{2,1,0:T(8,128)S(1)}, u32[]{:S(2)}, u32[]{:S(2)}) %all-to-all-start.1) | async-done | bytes 131104 | tf_op jit(solution)/shard_map/all_to_all | solution.py:567
  74.6 0.0 collective-permute-done.1.refs_8_
  74.6 0.0 copy-done
  74.6 0.0 copy-done.2
  74.6 0.0 copy-done.4
  74.6 0.0 copy-done.5
  74.6 0.0 copy-done.7
  74.6 3.8 %arnoldi_step.6 = (f32[256,128]{1,0:T(8,128)S(1)}, f32[8,128]{1,0:T(8,128)S(1)}, f32[32,8,128]{2,1,0:T(8,128)S(1)}, s32[8]{0:T(128)S(1)}, f32[1288,128]{1,0:T(8,128)S(1)}, /*index=5*/f32[32,16384]{1,0:T(8,128)S(1)}) custom-call(s32[2]{0:T(128)S(1)} %pad_add_fusion.place_ref.refs_0_, s32[16]{0:T(128)S(1)} %bitcast.39, ...), custom_call_target="tpu_custom_call" | custom-call | tf_op jit(solution)/shard_map/arnoldi_step/pallas_call | solution.py:455
  78.5 10.3 %all_to_all.40.refs_3_ = f32[32,8,128]{2,1,0:T(8,128)S(1)} all-to-all(f32[32,8,128]{2,1,0:T(8,128)S(1)} %get-tuple-element.34), channel_id=1, replica_groups=mesh['wake'=16,'col'=2] {'wake','col'}, dimensions={0} | all-to-all | bytes 262144 | tf_op jit(solution)/shard_map/all_to_all | solution.py:567
  88.8 1.8 %arnoldi_step.7 = (f32[256,128]{1,0:T(8,128)S(1)}, f32[8,128]{1,0:T(8,128)S(1)}, f32[32,8,128]{2,1,0:T(8,128)S(1)}) custom-call(s32[2]{0:T(128)S(1)} %pad_add_fusion.place_ref.refs_0_, s32[16]{0:T(128)S(1)} %bitcast.40, s32[8]{0:T(128)S(1)} %get-tuple-element.33.refs_2_, f32[32,8,128]{2,1,0:T(8,128)S(1)} %all_to_all.40.refs_3_, ...), custom_call_target="tpu_custom_call" | custom-call | tf_op jit(solution)/shard_map/arnoldi_step/pallas_call | solution.py:455
  90.6 10.3 %all_to_all.41.refs_3_ = f32[32,8,128]{2,1,0:T(8,128)S(1)} all-to-all(f32[32,8,128]{2,1,0:T(8,128)S(1)} %get-tuple-element.38), channel_id=1, replica_groups=mesh['wake'=16,'col'=2] {'wake','col'}, dimensions={0} | all-to-all | bytes 262144 | tf_op jit(solution)/shard_map/all_to_all | solution.py:567
  101.0 1.8 %arnoldi_step.8 = (f32[256,128]{1,0:T(8,128)S(1)}, f32[8,128]{1,0:T(8,128)S(1)}, f32[32,8,128]{2,1,0:T(8,128)S(1)}) custom-call(s32[2]{0:T(128)S(1)} %pad_add_fusion.place_ref.refs_0_, s32[16]{0:T(128)S(1)} %bitcast.41, s32[8]{0:T(128)S(1)} %get-tuple-element.33.refs_2_, f32[32,8,128]{2,1,0:T(8,128)S(1)} %all_to_all.41.refs_3_, ...), custom_call_target="tpu_custom_call" | custom-call | tf_op jit(solution)/shard_map/arnoldi_step/pallas_call | solution.py:455
  102.8 10.3 %all_to_all.42.refs_3_ = f32[32,8,128]{2,1,0:T(8,128)S(1)} all-to-all(f32[32,8,128]{2,1,0:T(8,128)S(1)} %get-tuple-element.40), channel_id=1, replica_groups=mesh['wake'=16,'col'=2] {'wake','col'}, dimensions={0} | all-to-all | bytes 262144 | tf_op jit(solution)/shard_map/all_to_all | solution.py:567
  113.1 1.9 %arnoldi_step.9 = (f32[256,128]{1,0:T(8,128)S(1)}, f32[8,128]{1,0:T(8,128)S(1)}, f32[32,8,128]{2,1,0:T(8,128)S(1)}) custom-call(s32[2]{0:T(128)S(1)} %pad_add_fusion.place_ref.refs_0_, s32[16]{0:T(128)S(1)} %bitcast.42, s32[8]{0:T(128)S(1)} %get-tuple-element.33.refs_2_, f32[32,8,128]{2,1,0:T(8,128)S(1)} %all_to_all.42.refs_3_, ...), custom_call_target="tpu_custom_call" | custom-call | tf_op jit(solution)/shard_map/arnoldi_step/pallas_call | solution.py:455
  115.0 10.3 %all_to_all.43.refs_3_ = f32[32,8,128]{2,1,0:T(8,128)S(1)} all-to-all(f32[32,8,128]{2,1,0:T(8,128)S(1)} %get-tuple-element.42), channel_id=1, replica_groups=mesh['wake'=16,'col'=2] {'wake','col'}, dimensions={0} | all-to-all | bytes 262144 | tf_op jit(solution)/shard_map/all_to_all | solution.py:567
  125.3 1.9 %arnoldi_step.10 = (f32[256,128]{1,0:T(8,128)S(1)}, f32[8,128]{1,0:T(8,128)S(1)}, f32[32,8,128]{2,1,0:T(8,128)S(1)}) custom-call(s32[2]{0:T(128)S(1)} %pad_add_fusion.place_ref.refs_0_, s32[16]{0:T(128)S(1)} %bitcast.43, s32[8]{0:T(128)S(1)} %get-tuple-element.33.refs_2_, f32[32,8,128]{2,1,0:T(8,128)S(1)} %all_to_all.43.refs_3_, ...), custom_call_target="tpu_custom_call" | custom-call | tf_op jit(solution)/shard_map/arnoldi_step/pallas_call | solution.py:455
  127.2 10.3 %all_to_all.44.refs_3_ = f32[32,8,128]{2,1,0:T(8,128)S(1)} all-to-all(f32[32,8,128]{2,1,0:T(8,128)S(1)} %get-tuple-element.44), channel_id=1, replica_groups=mesh['wake'=16,'col'=2] {'wake','col'}, dimensions={0} | all-to-all | bytes 262144 | tf_op jit(solution)/shard_map/all_to_all | solution.py:567
  137.5 1.9 %arnoldi_step.11 = (f32[256,128]{1,0:T(8,128)S(1)}, f32[8,128]{1,0:T(8,128)S(1)}, f32[32,8,128]{2,1,0:T(8,128)S(1)}) custom-call(s32[2]{0:T(128)S(1)} %pad_add_fusion.place_ref.refs_0_, s32[16]{0:T(128)S(1)} %bitcast.44, s32[8]{0:T(128)S(1)} %get-tuple-element.33.refs_2_, f32[32,8,128]{2,1,0:T(8,128)S(1)} %all_to_all.44.refs_3_, ...), custom_call_target="tpu_custom_call" | custom-call | tf_op jit(solution)/shard_map/arnoldi_step/pallas_call | solution.py:455
  139.4 10.3 %all_to_all.45.image_ref = f32[32,8,128]{2,1,0:T(8,128)S(1)} all-to-all(f32[32,8,128]{2,1,0:T(8,128)S(1)} %get-tuple-element.46), channel_id=1, replica_groups=mesh['wake'=16,'col'=2] {'wake','col'}, dimensions={0} | all-to-all | bytes 262144 | tf_op jit(solution)/shard_map/all_to_all | solution.py:573
  149.8 1.6 %finish.1 = f32[8,128]{1,0:T(8,128)} custom-call(s32[2]{0:T(128)S(1)} %pad_add_fusion.place_ref.refs_0_, f32[32,8,128]{2,1,0:T(8,128)S(1)} %all_to_all.45.image_ref, f32[256,128]{1,0:T(8,128)S(1)} %get-tuple-element.35.refs_4_.refs_0_, f32[256,128]{1,0:T(8,128)S(1)} %get-tuple-element.39.refs_5_.refs_1_, f32[256,128]{1,0:T(8,128)S(1)} %get-tuple-element.41.refs_6_.refs_2_, ...), custom_call_target="tpu_custom_call" | custom-call | tf_op jit(solution)/shard_map/finish/pallas_call | solution.py:520
Async XLA Ops:
  0.6 74.0 %collective-permute-start.1 = (f32[32,16384]{1,0:T(8,128)}, f32[32,16384]{1,0:T(8,128)}, u32[]{:S(2)}, u32[]{:S(2)}) collective-permute-start(f32[32,16384]{1,0:T(8,128)} %bitcast.11), channel_id=1, source_target_pairs={{0,1},{1,0},{2,3},{3,2},{4,5},{5,4},{6,7},{7,6},{8,9},{9,8},{10,11... | collective-permute-start | bytes 6291464 | tf_op jit(solution)/shard_map/ppermute | solution.py:557
  5.1 17.0 %all-to-all-start = ((f32[16,5,8,128]{3,2,1,0:T(8,128)}), f32[16,5,8,128]{3,2,1,0:T(8,128)S(1)}, u32[]{:S(2)}, u32[]{:S(2)}) async-start(f32[16,5,8,128]{3,2,1,0:T(8,128)} %pack_nodes.1), calls=%async_computation | async-start | bytes 655360 | tf_op jit(solution)/shard_map/all_to_all | solution.py:562
  11.2 1.2 copy-start.1
  12.4 0.9 copy-start.3
  13.3 0.7 copy-start.6
  15.4 50.5 %collective-permute-start = (f32[1288,128]{1,0:T(8,128)}, f32[1288,128]{1,0:T(8,128)}, u32[]{:S(2)}, u32[]{:S(2)}) collective-permute-start(f32[1288,128]{1,0:T(8,128)} %deal.1), channel_id=1, source_target_pairs={{0,1},{1,0},{2,3},{3,2},{4,5},{5,4},{6,7},{7,6},{8,9},{9,8},{10,11... | collective-permute-start | bytes 1978376 | tf_op jit(solution)/shard_map/ppermute | solution.py:556
  22.2 0.7 copy-start.8
  22.9 51.7 %copy-start = (f32[1,32,16384]{2,1,0:T(8,128)S(1)}, f32[1,32,16384]{2,1,0:T(8,128)}, u32[]{:S(2)}) copy-start(f32[1,32,16384]{2,1,0:T(8,128)} %param.21) | copy-start | bytes 6291460
  22.9 51.7 %copy-start.2 = (f32[16,1,1,128,128]{4,3,2,1,0:T(8,128)S(1)}, f32[16,1,1,128,128]{4,3,2,1,0:T(8,128)}, u32[]{:S(2)}) copy-start(f32[16,1,1,128,128]{4,3,2,1,0:T(8,128)} %param.18) | copy-start | bytes 3145732
  22.9 51.7 %copy-start.4 = (f32[1,32,2048]{2,1,0:T(8,128)S(1)}, f32[1,32,2048]{2,1,0:T(8,128)}, u32[]{:S(2)}) copy-start(f32[1,32,2048]{2,1,0:T(8,128)} %param.20) | copy-start | bytes 786436
  22.9 51.7 %copy-start.5 = (f32[1024]{0:T(1024)S(1)}, f32[1024]{0:T(1024)}, u32[]{:S(2)}) copy-start(f32[1024]{0:T(1024)} %param.17) | copy-start | bytes 12292
  22.9 51.7 %copy-start.7 = (s32[16,1,1]{0,2,1:T(1,128)S(1)}, s32[16,1,1]{0,2,1:T(1,128)}, u32[]{:S(2)}) copy-start(s32[16,1,1]{0,2,1:T(1,128)} %param.19) | copy-start | bytes 196
  63.4 11.2 %all-to-all-start.1 = ((f32[32,8,128]{2,1,0:T(8,128)}), f32[32,8,128]{2,1,0:T(8,128)S(1)}, u32[]{:S(2)}, u32[]{:S(2)}) async-start(f32[32,8,128]{2,1,0:T(8,128)} %get-tuple-element.32), calls=%async_computation.1 | async-start | bytes 262144 | tf_op jit(solution)/shard_map/all_to_all | solution.py:567

commit v4 on v3

--- a/solution.py
+++ b/solution.py
@@ -20,8 +20,8 @@
 WIDE = 2 * LANES
 HALF = LANES // 2
 BLOCKS = HALF // RUN
-PANEL_STEP = 256
-BLOCK_STEP = 8
+PANEL_STEP = 128
+BLOCK_STEP = 16
 
 VMEM = pl.BlockSpec(memory_space=pltpu.VMEM)
 SMEM = pl.BlockSpec(memory_space=pltpu.SMEM)
@@ -144,7 +144,7 @@
 def induce_kernel(
     nodes_in, normal_side_in, length_side_in, info_in, right_ref, copies_ref,
     nodes_ref, normal_side_ref, length_side_ref, info_ref,
-    normal_ref, length_ref, inner_ref, normal_pick_ref, length_pick_ref, total_ref, arrived,
+    normal_ref, length_ref, square_ref, normal_pick_ref, length_pick_ref, total_ref, arrived,
 ):
     fetches = [
         pltpu.make_async_copy(source, target, arrived.at[i])
@@ -170,7 +170,7 @@
     turned = pltpu.roll(tag, LANES - 1, 1)
     next_tag = jnp.where(lane == LANES - 1, pltpu.roll(turned, rows - 1, 0), turned)
     linked = (tag == next_tag) & ((lane < LANES - 1) | (row < rows - 1))
-    strength = jnp.where(linked, circulation * (1.0 / FOUR_PI), 0.0)
+    strength = jnp.where(linked, circulation * (2.0 / FOUR_PI), 0.0)
     runs = [
         [
             (value - info_ref[piece_rows + q : piece_rows + q + 1, :])[g * LANES : (g + 1) * LANES].T
@@ -218,8 +218,9 @@
             rows = [pieces[k][p] for _, p in LENGTH_PRODUCTS for k in range(3)]
             return rows + [ones] * 3 + list(three_pieces(square))
 
-        inner = length_rows([-(a[q] + b[q]) for q in range(3)], a[0] * b[0] + a[1] * b[1] + a[2] * b[2])
-        put(inner_ref, inner, BLOCKS)
+        square = sum((a[q] - b[q]) * (a[q] - b[q]) for q in range(3))
+        for half in range(2):
+            square_ref[:, half * LANES : (half + 1) * LANES] = square[half * HALF : (half + 1) * HALF]
         after = length_rows([-2.0 * b[q] for q in range(3)], b[0] * b[0] + b[1] * b[1] + b[2] * b[2])
         put(length_ref, after, BLOCKS)
         start = length_rows([-2.0 * a[q] for q in range(3)], a[0] * a[0] + a[1] * a[1] + a[2] * a[2])
@@ -249,11 +250,11 @@
                     block = step * BLOCK_STEP + i
                     for j in range(RUN):
                         normal_part = form(normal_pick_ref, j, normal_ref[block])
-                        inner = form(length_pick_ref, j, inner_ref[block])
                         after = length_of(form(length_pick_ref, j, length_ref[block]))
-                        product = length * after
-                        below = product * (product + inner) + CORE_SQ
-                        total = total + ((length + after) * normal_part) * pl.reciprocal(below)
+                        reach = length + after
+                        gap = reach * reach - square_ref[pl.ds(block * RUN + j, 1), :]
+                        below = (length * after) * gap + 2.0 * CORE_SQ
+                        total = total + (reach * normal_part) * pl.reciprocal(below)
                         length = after
                 return length, total
 
@@ -294,7 +295,7 @@
             pltpu.VMEM((piece_rows + 8, LANES), jnp.float32),
             pltpu.VMEM((BLOCKS, DEPTH, WIDE), jnp.bfloat16),
             pltpu.VMEM((BLOCKS + 1, DEPTH, WIDE), jnp.bfloat16),
-            pltpu.VMEM((BLOCKS, DEPTH, WIDE), jnp.bfloat16),
+            pltpu.VMEM((HALF, WIDE), jnp.float32),
             pltpu.VMEM((RUN, PANEL_STEP, DEPTH), jnp.bfloat16),
             pltpu.VMEM((RUN, PANEL_STEP, DEPTH), jnp.bfloat16),
             pltpu.VMEM((piece, LANES), jnp.float32),

time: 152 us -> 148 us (0.974)
  Pallas kernels: 60.2 us -> 56.7 us
    pallas_call x1, Pallas kernels: 40.4 us -> 36.9 us  [induce(): pl.pallas_call(induce_kernel, out_shape=(jax.ShapeDtypeStruct((piece_rows...]
  transfers between devices with their start and end apart: 4 -> 4, of which waited for: 2 -> 3; matrix products, arithmetic and copies ran while one was open for 0% -> 0% of each run, Pallas kernels for 30% -> 28%
where the time goes in v4:
time: 148 us
  blocking collectives  62 us (42%)
  Pallas kernels  56.7 us (38%)
  waiting for transfers between devices  12.7 us (9%)
  starting transfers between devices  12.1 us (8%)
  local copies, waits for them, and re-layouts  3.59 us (2%)
    all_to_all x6, blocking collectives, body(): image = lax.all_to_all(image_copies, everyone, 0, 0, tiled=True)  62 us
    pallas_call x1, Pallas kernels, induce(): pl.pallas_call(induce_kernel, out_shape=(jax.ShapeDtypeStruct((piece_rows...  36.9 us
    pallas_call x6, Pallas kernels, arnoldi_step(): pl.pallas_call(functools.partial(step_kernel, len(known), 1 + len(dealt),...  13.1 us
    all_to_all x1, waiting for transfers between devices, body(): image = lax.all_to_all(image_copies, everyone, 0, 0, tiled=True)  7.32 us
    all_to_all x1, starting transfers between devices, body(): nodes = lax.all_to_all(packed, 'wake', 0, 0, tiled=True)  5.94 us
    all_to_all x1, waiting for transfers between devices, body(): nodes = lax.all_to_all(packed, 'wake', 0, 0, tiled=True)  4.04 us
    unnamed x18, local copies, waits for them, and re-layouts  3.59 us
    ppermute x1, starting transfers between devices, body(): rights.append(lax.ppermute(right, 'col', pairs))  3 us
  transfers between devices with their start and end apart: 4, of which 3 were waited for; matrix products, arithmetic and copies ran while one was open for 0% of the time, Pallas kernels for 28%

profile of v4, /device:TPU:0, one launch (start us, length us, event | category | flops | bytes accessed | tf_op | source)
XLA Modules:
  0.0 147.8 jit_solution(11172669535722378263)
XLA Ops:
  0.6 3.0 %collective-permute-start.1 = (f32[32,16384]{1,0:T(8,128)}, f32[32,16384]{1,0:T(8,128)}, u32[]{:S(2)}, u32[]{:S(2)}) collective-permute-start(f32[32,16384]{1,0:T(8,128)} %bitcast.11), channel_id=1, source_target_pairs={{0,1},{1,0},{2,3},{3,2},{4,5},{5,4},{6,7},{7,6},{8,9},{9,8},{10,11... | collective-permute-start | bytes 6291464 | tf_op jit(solution)/shard_map/ppermute | solution.py:558
  3.6 1.5 %pack_nodes.1 = f32[16,5,8,128]{3,2,1,0:T(8,128)} custom-call(f32[3,1024]{1,0:T(4,128)} %nodes_ref.1, f32[8,128]{1,0:T(8,128)} %bitcast.45, s32[8,128]{1,0:T(8,128)} %bitcast.46), custom_call_target="tpu_custom_call" | custom-call | tf_op jit(solution)/shard_map/pack_nodes/pallas_call | solution.py:46
  5.1 5.9 %all-to-all-start = ((f32[16,5,8,128]{3,2,1,0:T(8,128)}), f32[16,5,8,128]{3,2,1,0:T(8,128)S(1)}, u32[]{:S(2)}, u32[]{:S(2)}) async-start(f32[16,5,8,128]{3,2,1,0:T(8,128)} %pack_nodes.1), calls=%async_computation | async-start | bytes 655360 | tf_op jit(solution)/shard_map/all_to_all | solution.py:563
  11.1 0.1 pad_add_fusion.place_ref.refs_0_
  11.2 0.0 copy-start.1
  11.2 1.2 copy-done.1
  12.4 0.0 copy-start.3
  12.4 0.9 copy-done.3
  13.3 0.0 copy-start.6
  13.3 0.7 copy-done.6
  14.0 1.4 deal.1
  15.4 0.5 collective-permute-start
  16.0 2.2 %prepare_panels.1 = (bf16[1024,128]{1,0:T(8,128)(2,1)}, bf16[1024,128]{1,0:T(8,128)(2,1)}, f32[16,128]{1,0:T(8,128)}) custom-call(f32[3,1024]{1,0:T(4,128)} %points_ref.1, f32[3,1024]{1,0:T(4,128)} %normals_ref.1, f32[3]{0:T(128)} %stream_ref.1), custom_call_target="tpu_custom_call" | custom-call | tf_op jit(solution)/shard_map/prepare_panels/pallas_call | solution.py:125
  18.1 4.0 %all-to-all-done.nodes_in = f32[16,5,8,128]{3,2,1,0:T(8,128)S(1)} async-done(((f32[16,5,8,128]{3,2,1,0:T(8,128)}), f32[16,5,8,128]{3,2,1,0:T(8,128)S(1)}, u32[]{:S(2)}, u32[]{:S(2)}) %all-to-all-start) | async-done | bytes 327712 | tf_op jit(solution)/shard_map/all_to_all | solution.py:563
  22.2 0.0 copy-start.8
  22.2 0.7 copy-done.8
  22.9 0.0 copy-start
  22.9 0.0 copy-start.2
  22.9 0.0 copy-start.4
  22.9 0.0 copy-start.5
  22.9 0.0 copy-start.7
  23.0 36.9 %induce.1 = (f32[8,128]{1,0:T(8,128)}, f32[32,8,128]{2,1,0:T(8,128)}) custom-call(f32[16,5,8,128]{3,2,1,0:T(8,128)} %copy-done.8, bf16[1024,128]{1,0:T(8,128)(2,1)} %get-tuple-element.28.normal_side_in, bf16[1024,128]{1,0:T(8,128)(2,1)} %get-tuple-element.29.length_side_in, f32[16,128]{1,0:T(8,128)} %get-tuple-element.30.info_in), custom_call_target="tpu_custom_call" | custom-call | flops 503316480 | bytes 2097152 | tf_op jit(solution)/shard_map/induce/pallas_call | solution.py:283
  59.8 2.6 %all-to-all-start.1 = ((f32[32,8,128]{2,1,0:T(8,128)}), f32[32,8,128]{2,1,0:T(8,128)S(1)}, u32[]{:S(2)}, u32[]{:S(2)}) async-start(f32[32,8,128]{2,1,0:T(8,128)} %get-tuple-element.32), calls=%async_computation.1 | async-start | bytes 262144 | tf_op jit(solution)/shard_map/all_to_all | solution.py:568
  62.4 1.3 collective-permute-done.refs_7_
  63.7 7.3 %all-to-all-done.1.refs_2_ = f32[32,8,128]{2,1,0:T(8,128)S(1)} async-done(((f32[32,8,128]{2,1,0:T(8,128)}), f32[32,8,128]{2,1,0:T(8,128)S(1)}, u32[]{:S(2)}, u32[]{:S(2)}) %all-to-all-start.1) | async-done | bytes 131104 | tf_op jit(solution)/shard_map/all_to_all | solution.py:568
  71.0 0.0 collective-permute-done.1.refs_8_
  71.0 0.0 copy-done
  71.0 0.0 copy-done.2
  71.0 0.0 copy-done.4
  71.1 0.0 copy-done.5
  71.1 0.0 copy-done.7
  71.1 3.8 %arnoldi_step.6 = (f32[256,128]{1,0:T(8,128)S(1)}, f32[8,128]{1,0:T(8,128)S(1)}, f32[32,8,128]{2,1,0:T(8,128)S(1)}, s32[8]{0:T(128)S(1)}, f32[1288,128]{1,0:T(8,128)S(1)}, /*index=5*/f32[32,16384]{1,0:T(8,128)S(1)}) custom-call(s32[2]{0:T(128)S(1)} %pad_add_fusion.place_ref.refs_0_, s32[16]{0:T(128)S(1)} %bitcast.39, ...), custom_call_target="tpu_custom_call" | custom-call | tf_op jit(solution)/shard_map/arnoldi_step/pallas_call | solution.py:456
  74.9 10.3 %all_to_all.40.refs_3_ = f32[32,8,128]{2,1,0:T(8,128)S(1)} all-to-all(f32[32,8,128]{2,1,0:T(8,128)S(1)} %get-tuple-element.34), channel_id=1, replica_groups=mesh['wake'=16,'col'=2] {'wake','col'}, dimensions={0} | all-to-all | bytes 262144 | tf_op jit(solution)/shard_map/all_to_all | solution.py:568
  85.2 1.8 %arnoldi_step.7 = (f32[256,128]{1,0:T(8,128)S(1)}, f32[8,128]{1,0:T(8,128)S(1)}, f32[32,8,128]{2,1,0:T(8,128)S(1)}) custom-call(s32[2]{0:T(128)S(1)} %pad_add_fusion.place_ref.refs_0_, s32[16]{0:T(128)S(1)} %bitcast.40, s32[8]{0:T(128)S(1)} %get-tuple-element.33.refs_2_, f32[32,8,128]{2,1,0:T(8,128)S(1)} %all_to_all.40.refs_3_, ...), custom_call_target="tpu_custom_call" | custom-call | tf_op jit(solution)/shard_map/arnoldi_step/pallas_call | solution.py:456
  87.1 10.3 %all_to_all.41.refs_3_ = f32[32,8,128]{2,1,0:T(8,128)S(1)} all-to-all(f32[32,8,128]{2,1,0:T(8,128)S(1)} %get-tuple-element.38), channel_id=1, replica_groups=mesh['wake'=16,'col'=2] {'wake','col'}, dimensions={0} | all-to-all | bytes 262144 | tf_op jit(solution)/shard_map/all_to_all | solution.py:568
  97.4 1.8 %arnoldi_step.8 = (f32[256,128]{1,0:T(8,128)S(1)}, f32[8,128]{1,0:T(8,128)S(1)}, f32[32,8,128]{2,1,0:T(8,128)S(1)}) custom-call(s32[2]{0:T(128)S(1)} %pad_add_fusion.place_ref.refs_0_, s32[16]{0:T(128)S(1)} %bitcast.41, s32[8]{0:T(128)S(1)} %get-tuple-element.33.refs_2_, f32[32,8,128]{2,1,0:T(8,128)S(1)} %all_to_all.41.refs_3_, ...), custom_call_target="tpu_custom_call" | custom-call | tf_op jit(solution)/shard_map/arnoldi_step/pallas_call | solution.py:456
  99.2 10.3 %all_to_all.42.refs_3_ = f32[32,8,128]{2,1,0:T(8,128)S(1)} all-to-all(f32[32,8,128]{2,1,0:T(8,128)S(1)} %get-tuple-element.40), channel_id=1, replica_groups=mesh['wake'=16,'col'=2] {'wake','col'}, dimensions={0} | all-to-all | bytes 262144 | tf_op jit(solution)/shard_map/all_to_all | solution.py:568
  109.6 1.9 %arnoldi_step.9 = (f32[256,128]{1,0:T(8,128)S(1)}, f32[8,128]{1,0:T(8,128)S(1)}, f32[32,8,128]{2,1,0:T(8,128)S(1)}) custom-call(s32[2]{0:T(128)S(1)} %pad_add_fusion.place_ref.refs_0_, s32[16]{0:T(128)S(1)} %bitcast.42, s32[8]{0:T(128)S(1)} %get-tuple-element.33.refs_2_, f32[32,8,128]{2,1,0:T(8,128)S(1)} %all_to_all.42.refs_3_, ...), custom_call_target="tpu_custom_call" | custom-call | tf_op jit(solution)/shard_map/arnoldi_step/pallas_call | solution.py:456
  111.4 10.3 %all_to_all.43.refs_3_ = f32[32,8,128]{2,1,0:T(8,128)S(1)} all-to-all(f32[32,8,128]{2,1,0:T(8,128)S(1)} %get-tuple-element.42), channel_id=1, replica_groups=mesh['wake'=16,'col'=2] {'wake','col'}, dimensions={0} | all-to-all | bytes 262144 | tf_op jit(solution)/shard_map/all_to_all | solution.py:568
  121.8 1.9 %arnoldi_step.10 = (f32[256,128]{1,0:T(8,128)S(1)}, f32[8,128]{1,0:T(8,128)S(1)}, f32[32,8,128]{2,1,0:T(8,128)S(1)}) custom-call(s32[2]{0:T(128)S(1)} %pad_add_fusion.place_ref.refs_0_, s32[16]{0:T(128)S(1)} %bitcast.43, s32[8]{0:T(128)S(1)} %get-tuple-element.33.refs_2_, f32[32,8,128]{2,1,0:T(8,128)S(1)} %all_to_all.43.refs_3_, ...), custom_call_target="tpu_custom_call" | custom-call | tf_op jit(solution)/shard_map/arnoldi_step/pallas_call | solution.py:456
  123.6 10.3 %all_to_all.44.refs_3_ = f32[32,8,128]{2,1,0:T(8,128)S(1)} all-to-all(f32[32,8,128]{2,1,0:T(8,128)S(1)} %get-tuple-element.44), channel_id=1, replica_groups=mesh['wake'=16,'col'=2] {'wake','col'}, dimensions={0} | all-to-all | bytes 262144 | tf_op jit(solution)/shard_map/all_to_all | solution.py:568
  134.0 1.9 %arnoldi_step.11 = (f32[256,128]{1,0:T(8,128)S(1)}, f32[8,128]{1,0:T(8,128)S(1)}, f32[32,8,128]{2,1,0:T(8,128)S(1)}) custom-call(s32[2]{0:T(128)S(1)} %pad_add_fusion.place_ref.refs_0_, s32[16]{0:T(128)S(1)} %bitcast.44, s32[8]{0:T(128)S(1)} %get-tuple-element.33.refs_2_, f32[32,8,128]{2,1,0:T(8,128)S(1)} %all_to_all.44.refs_3_, ...), custom_call_target="tpu_custom_call" | custom-call | tf_op jit(solution)/shard_map/arnoldi_step/pallas_call | solution.py:456
  135.9 10.3 %all_to_all.45.image_ref = f32[32,8,128]{2,1,0:T(8,128)S(1)} all-to-all(f32[32,8,128]{2,1,0:T(8,128)S(1)} %get-tuple-element.46), channel_id=1, replica_groups=mesh['wake'=16,'col'=2] {'wake','col'}, dimensions={0} | all-to-all | bytes 262144 | tf_op jit(solution)/shard_map/all_to_all | solution.py:574
  146.2 1.6 %finish.1 = f32[8,128]{1,0:T(8,128)} custom-call(s32[2]{0:T(128)S(1)} %pad_add_fusion.place_ref.refs_0_, f32[32,8,128]{2,1,0:T(8,128)S(1)} %all_to_all.45.image_ref, f32[256,128]{1,0:T(8,128)S(1)} %get-tuple-element.35.refs_4_.refs_0_, f32[256,128]{1,0:T(8,128)S(1)} %get-tuple-element.39.refs_5_.refs_1_, f32[256,128]{1,0:T(8,128)S(1)} %get-tuple-element.41.refs_6_.refs_2_, ...), custom_call_target="tpu_custom_call" | custom-call | tf_op jit(solution)/shard_map/finish/pallas_call | solution.py:521
Async XLA Ops:
  0.6 70.4 %collective-permute-start.1 = (f32[32,16384]{1,0:T(8,128)}, f32[32,16384]{1,0:T(8,128)}, u32[]{:S(2)}, u32[]{:S(2)}) collective-permute-start(f32[32,16384]{1,0:T(8,128)} %bitcast.11), channel_id=1, source_target_pairs={{0,1},{1,0},{2,3},{3,2},{4,5},{5,4},{6,7},{7,6},{8,9},{9,8},{10,11... | collective-permute-start | bytes 6291464 | tf_op jit(solution)/shard_map/ppermute | solution.py:558
  5.1 17.0 %all-to-all-start = ((f32[16,5,8,128]{3,2,1,0:T(8,128)}), f32[16,5,8,128]{3,2,1,0:T(8,128)S(1)}, u32[]{:S(2)}, u32[]{:S(2)}) async-start(f32[16,5,8,128]{3,2,1,0:T(8,128)} %pack_nodes.1), calls=%async_computation | async-start | bytes 655360 | tf_op jit(solution)/shard_map/all_to_all | solution.py:563
  11.2 1.2 copy-start.1
  12.4 0.9 copy-start.3
  13.3 0.7 copy-start.6
  15.4 48.3 %collective-permute-start = (f32[1288,128]{1,0:T(8,128)}, f32[1288,128]{1,0:T(8,128)}, u32[]{:S(2)}, u32[]{:S(2)}) collective-permute-start(f32[1288,128]{1,0:T(8,128)} %deal.1), channel_id=1, source_target_pairs={{0,1},{1,0},{2,3},{3,2},{4,5},{5,4},{6,7},{7,6},{8,9},{9,8},{10,11... | collective-permute-start | bytes 1978376 | tf_op jit(solution)/shard_map/ppermute | solution.py:557
  22.2 0.7 copy-start.8
  22.9 48.1 %copy-start = (f32[1,32,16384]{2,1,0:T(8,128)S(1)}, f32[1,32,16384]{2,1,0:T(8,128)}, u32[]{:S(2)}) copy-start(f32[1,32,16384]{2,1,0:T(8,128)} %param.21) | copy-start | bytes 6291460
  22.9 48.1 %copy-start.2 = (f32[16,1,1,128,128]{4,3,2,1,0:T(8,128)S(1)}, f32[16,1,1,128,128]{4,3,2,1,0:T(8,128)}, u32[]{:S(2)}) copy-start(f32[16,1,1,128,128]{4,3,2,1,0:T(8,128)} %param.18) | copy-start | bytes 3145732
  22.9 48.1 %copy-start.4 = (f32[1,32,2048]{2,1,0:T(8,128)S(1)}, f32[1,32,2048]{2,1,0:T(8,128)}, u32[]{:S(2)}) copy-start(f32[1,32,2048]{2,1,0:T(8,128)} %param.20) | copy-start | bytes 786436
  22.9 48.1 %copy-start.5 = (f32[1024]{0:T(1024)S(1)}, f32[1024]{0:T(1024)}, u32[]{:S(2)}) copy-start(f32[1024]{0:T(1024)} %param.17) | copy-start | bytes 12292
  22.9 48.1 %copy-start.7 = (s32[16,1,1]{0,2,1:T(1,128)S(1)}, s32[16,1,1]{0,2,1:T(1,128)}, u32[]{:S(2)}) copy-start(s32[16,1,1]{0,2,1:T(1,128)} %param.19) | copy-start | bytes 196
  59.8 11.2 %all-to-all-start.1 = ((f32[32,8,128]{2,1,0:T(8,128)}), f32[32,8,128]{2,1,0:T(8,128)S(1)}, u32[]{:S(2)}, u32[]{:S(2)}) async-start(f32[32,8,128]{2,1,0:T(8,128)} %get-tuple-element.32), calls=%async_computation.1 | async-start | bytes 262144 | tf_op jit(solution)/shard_map/all_to_all | solution.py:568

commit v5 on v4

--- a/solution.py
+++ b/solution.py
@@ -551,14 +551,14 @@
     place = jnp.stack([lax.axis_index("wake") * n_col + mine, mine])
 
     near, index, left, right = near_blocks[:, 0, 0], near_index[:, 0, 0], far_left[0], far_right[0]
+    packed, sent = lax.optimization_barrier((pack_nodes(wake_nodes, circulation, filament, n_wake), right))
     dealt, rights = [], []
     for shift, part in enumerate(deal(place, index, near, left, n_col), 1):
         pairs = [(source, (source + shift) % n_col) for source in range(n_col)]
         dealt.append(lax.ppermute(part, "col", pairs))
-        rights.append(lax.ppermute(right, "col", pairs))
+        rights.append(lax.ppermute(sent, "col", pairs))
     others = (dealt, rights)
 
-    packed = pack_nodes(wake_nodes, circulation, filament, n_wake)
     panels = prepare_panels(points, normals, freestream)
     nodes = lax.all_to_all(packed, "wake", 0, 0, tiled=True)
     right_side, image_copies = induce(nodes, panels, copies)

time: 148 us -> 148 us (level)
    all_to_all x1, waiting for transfers between devices: 7.32 us -> 5.75 us  [body(): image = lax.all_to_all(image_copies, everyone, 0, 0, tiled=True)]
    ppermute x1, waiting for transfers between devices: 1.3 us -> 2.87 us  [body(): dealt.append(lax.ppermute(part, 'col', pairs))]
  transfers between devices with their start and end apart: 4 -> 4, of which waited for: 3 -> 3; matrix products, arithmetic and copies ran while one was open for 0% -> 0% of each run, Pallas kernels for 28% -> 27%
where the time goes in v5:
time: 148 us
  blocking collectives  62 us (42%)
  Pallas kernels  56.6 us (38%)
  waiting for transfers between devices  12.7 us (9%)
  starting transfers between devices  12 us (8%)
  local copies, waits for them, and re-layouts  3.59 us (2%)
    all_to_all x6, blocking collectives, body(): image = lax.all_to_all(image_copies, everyone, 0, 0, tiled=True)  62 us
    pallas_call x1, Pallas kernels, induce(): pl.pallas_call(induce_kernel, out_shape=(jax.ShapeDtypeStruct((piece_rows...  36.8 us
    pallas_call x6, Pallas kernels, arnoldi_step(): pl.pallas_call(functools.partial(step_kernel, len(known), 1 + len(dealt),...  13.1 us
    all_to_all x1, starting transfers between devices, body(): nodes = lax.all_to_all(packed, 'wake', 0, 0, tiled=True)  5.94 us
    all_to_all x1, waiting for transfers between devices, body(): image = lax.all_to_all(image_copies, everyone, 0, 0, tiled=True)  5.75 us
    all_to_all x1, waiting for transfers between devices, body(): nodes = lax.all_to_all(packed, 'wake', 0, 0, tiled=True)  4.04 us
    unnamed x18, local copies, waits for them, and re-layouts  3.59 us
  transfers between devices with their start and end apart: 4, of which 3 were waited for; matrix products, arithmetic and copies ran while one was open for 0% of the time, Pallas kernels for 27%

profile of v5, /device:TPU:0, one launch (start us, length us, event | category | flops | bytes accessed | tf_op | source)
XLA Modules:
  0.0 147.7 jit_solution(10710863688409456496)
XLA Ops:
  0.6 1.5 %pack_nodes.1 = f32[16,5,8,128]{3,2,1,0:T(8,128)} custom-call(f32[3,1024]{1,0:T(4,128)} %nodes_ref.1, f32[8,128]{1,0:T(8,128)} %bitcast.45, s32[8,128]{1,0:T(8,128)} %bitcast.46), custom_call_target="tpu_custom_call" | custom-call | tf_op jit(solution)/shard_map/pack_nodes/pallas_call | solution.py:46
  2.1 2.9 %collective-permute-start.1 = (f32[32,16384]{1,0:T(8,128)}, f32[32,16384]{1,0:T(8,128)}, u32[]{:S(2)}, u32[]{:S(2)}) collective-permute-start(f32[32,16384]{1,0:T(8,128)} %bitcast.11), channel_id=1, source_target_pairs={{0,1},{1,0},{2,3},{3,2},{4,5},{5,4},{6,7},{7,6},{8,9},{9,8},{10,11... | collective-permute-start | bytes 6291464 | tf_op jit(solution)/shard_map/ppermute | solution.py:559
  5.1 5.9 %all-to-all-start = ((f32[16,5,8,128]{3,2,1,0:T(8,128)}), f32[16,5,8,128]{3,2,1,0:T(8,128)S(1)}, u32[]{:S(2)}, u32[]{:S(2)}) async-start(f32[16,5,8,128]{3,2,1,0:T(8,128)} %pack_nodes.1), calls=%async_computation | async-start | bytes 655360 | tf_op jit(solution)/shard_map/all_to_all | solution.py:563
  11.0 0.1 pad_add_fusion.place_ref.refs_0_
  11.1 0.0 copy-start.1
  11.1 1.2 copy-done.1
  12.3 0.0 copy-start.3
  12.3 0.9 copy-done.3
  13.3 0.0 copy-start.6
  13.3 0.7 copy-done.6
  13.9 1.4 deal.1
  15.4 0.5 collective-permute-start
  15.9 2.2 %prepare_panels.1 = (bf16[1024,128]{1,0:T(8,128)(2,1)}, bf16[1024,128]{1,0:T(8,128)(2,1)}, f32[16,128]{1,0:T(8,128)}) custom-call(f32[3,1024]{1,0:T(4,128)} %points_ref.1, f32[3,1024]{1,0:T(4,128)} %normals_ref.1, f32[3]{0:T(128)} %stream_ref.1), custom_call_target="tpu_custom_call" | custom-call | tf_op jit(solution)/shard_map/prepare_panels/pallas_call | solution.py:125
  18.1 4.0 %all-to-all-done.nodes_in = f32[16,5,8,128]{3,2,1,0:T(8,128)S(1)} async-done(((f32[16,5,8,128]{3,2,1,0:T(8,128)}), f32[16,5,8,128]{3,2,1,0:T(8,128)S(1)}, u32[]{:S(2)}, u32[]{:S(2)}) %all-to-all-start) | async-done | bytes 327712 | tf_op jit(solution)/shard_map/all_to_all | solution.py:563
  22.1 0.0 copy-start.8
  22.1 0.7 copy-done.8
  22.9 0.0 copy-start
  22.9 0.0 copy-start.2
  22.9 0.0 copy-start.4
  22.9 0.0 copy-start.5
  22.9 0.0 copy-start.7
  22.9 36.8 %induce.1 = (f32[8,128]{1,0:T(8,128)}, f32[32,8,128]{2,1,0:T(8,128)}) custom-call(f32[16,5,8,128]{3,2,1,0:T(8,128)} %copy-done.8, bf16[1024,128]{1,0:T(8,128)(2,1)} %get-tuple-element.31.normal_side_in, bf16[1024,128]{1,0:T(8,128)(2,1)} %get-tuple-element.32.length_side_in, f32[16,128]{1,0:T(8,128)} %get-tuple-element.33.info_in), custom_call_target="tpu_custom_call" | custom-call | flops 503316480 | bytes 2097152 | tf_op jit(solution)/shard_map/induce/pallas_call | solution.py:283
  59.7 2.6 %all-to-all-start.1 = ((f32[32,8,128]{2,1,0:T(8,128)}), f32[32,8,128]{2,1,0:T(8,128)S(1)}, u32[]{:S(2)}, u32[]{:S(2)}) async-start(f32[32,8,128]{2,1,0:T(8,128)} %get-tuple-element.35), calls=%async_computation.1 | async-start | bytes 262144 | tf_op jit(solution)/shard_map/all_to_all | solution.py:568
  62.3 2.9 %collective-permute-done.refs_7_ = f32[1288,128]{1,0:T(8,128)} collective-permute-done((f32[1288,128]{1,0:T(8,128)}, f32[1288,128]{1,0:T(8,128)}, u32[]{:S(2)}, u32[]{:S(2)}) %collective-permute-start) | collective-permute-done | bytes 659488 | tf_op jit(solution)/shard_map/ppermute | solution.py:558
  65.2 5.8 %all-to-all-done.1.refs_2_ = f32[32,8,128]{2,1,0:T(8,128)S(1)} async-done(((f32[32,8,128]{2,1,0:T(8,128)}), f32[32,8,128]{2,1,0:T(8,128)S(1)}, u32[]{:S(2)}, u32[]{:S(2)}) %all-to-all-start.1) | async-done | bytes 131104 | tf_op jit(solution)/shard_map/all_to_all | solution.py:568
  70.9 0.0 collective-permute-done.1.refs_8_
  70.9 0.0 copy-done
  70.9 0.0 copy-done.2
  70.9 0.0 copy-done.4
  70.9 0.0 copy-done.5
  70.9 0.0 copy-done.7
  70.9 3.8 %arnoldi_step.6 = (f32[256,128]{1,0:T(8,128)S(1)}, f32[8,128]{1,0:T(8,128)S(1)}, f32[32,8,128]{2,1,0:T(8,128)S(1)}, s32[8]{0:T(128)S(1)}, f32[1288,128]{1,0:T(8,128)S(1)}, /*index=5*/f32[32,16384]{1,0:T(8,128)S(1)}) custom-call(s32[2]{0:T(128)S(1)} %pad_add_fusion.place_ref.refs_0_, s32[16]{0:T(128)S(1)} %bitcast.39, ...), custom_call_target="tpu_custom_call" | custom-call | tf_op jit(solution)/shard_map/arnoldi_step/pallas_call | solution.py:456
  74.8 10.3 %all_to_all.40.refs_3_ = f32[32,8,128]{2,1,0:T(8,128)S(1)} all-to-all(f32[32,8,128]{2,1,0:T(8,128)S(1)} %get-tuple-element.38), channel_id=1, replica_groups=mesh['wake'=16,'col'=2] {'wake','col'}, dimensions={0} | all-to-all | bytes 262144 | tf_op jit(solution)/shard_map/all_to_all | solution.py:568
  85.1 1.8 %arnoldi_step.7 = (f32[256,128]{1,0:T(8,128)S(1)}, f32[8,128]{1,0:T(8,128)S(1)}, f32[32,8,128]{2,1,0:T(8,128)S(1)}) custom-call(s32[2]{0:T(128)S(1)} %pad_add_fusion.place_ref.refs_0_, s32[16]{0:T(128)S(1)} %bitcast.40, s32[8]{0:T(128)S(1)} %get-tuple-element.37.refs_2_, f32[32,8,128]{2,1,0:T(8,128)S(1)} %all_to_all.40.refs_3_, ...), custom_call_target="tpu_custom_call" | custom-call | tf_op jit(solution)/shard_map/arnoldi_step/pallas_call | solution.py:456
  86.9 10.3 %all_to_all.41.refs_3_ = f32[32,8,128]{2,1,0:T(8,128)S(1)} all-to-all(f32[32,8,128]{2,1,0:T(8,128)S(1)} %get-tuple-element.42), channel_id=1, replica_groups=mesh['wake'=16,'col'=2] {'wake','col'}, dimensions={0} | all-to-all | bytes 262144 | tf_op jit(solution)/shard_map/all_to_all | solution.py:568
  97.3 1.8 %arnoldi_step.8 = (f32[256,128]{1,0:T(8,128)S(1)}, f32[8,128]{1,0:T(8,128)S(1)}, f32[32,8,128]{2,1,0:T(8,128)S(1)}) custom-call(s32[2]{0:T(128)S(1)} %pad_add_fusion.place_ref.refs_0_, s32[16]{0:T(128)S(1)} %bitcast.41, s32[8]{0:T(128)S(1)} %get-tuple-element.37.refs_2_, f32[32,8,128]{2,1,0:T(8,128)S(1)} %all_to_all.41.refs_3_, ...), custom_call_target="tpu_custom_call" | custom-call | tf_op jit(solution)/shard_map/arnoldi_step/pallas_call | solution.py:456
  99.1 10.3 %all_to_all.42.refs_3_ = f32[32,8,128]{2,1,0:T(8,128)S(1)} all-to-all(f32[32,8,128]{2,1,0:T(8,128)S(1)} %get-tuple-element.44), channel_id=1, replica_groups=mesh['wake'=16,'col'=2] {'wake','col'}, dimensions={0} | all-to-all | bytes 262144 | tf_op jit(solution)/shard_map/all_to_all | solution.py:568
  109.4 1.9 %arnoldi_step.9 = (f32[256,128]{1,0:T(8,128)S(1)}, f32[8,128]{1,0:T(8,128)S(1)}, f32[32,8,128]{2,1,0:T(8,128)S(1)}) custom-call(s32[2]{0:T(128)S(1)} %pad_add_fusion.place_ref.refs_0_, s32[16]{0:T(128)S(1)} %bitcast.42, s32[8]{0:T(128)S(1)} %get-tuple-element.37.refs_2_, f32[32,8,128]{2,1,0:T(8,128)S(1)} %all_to_all.42.refs_3_, ...), custom_call_target="tpu_custom_call" | custom-call | tf_op jit(solution)/shard_map/arnoldi_step/pallas_call | solution.py:456
  111.3 10.3 %all_to_all.43.refs_3_ = f32[32,8,128]{2,1,0:T(8,128)S(1)} all-to-all(f32[32,8,128]{2,1,0:T(8,128)S(1)} %get-tuple-element.46), channel_id=1, replica_groups=mesh['wake'=16,'col'=2] {'wake','col'}, dimensions={0} | all-to-all | bytes 262144 | tf_op jit(solution)/shard_map/all_to_all | solution.py:568
  121.6 1.9 %arnoldi_step.10 = (f32[256,128]{1,0:T(8,128)S(1)}, f32[8,128]{1,0:T(8,128)S(1)}, f32[32,8,128]{2,1,0:T(8,128)S(1)}) custom-call(s32[2]{0:T(128)S(1)} %pad_add_fusion.place_ref.refs_0_, s32[16]{0:T(128)S(1)} %bitcast.43, s32[8]{0:T(128)S(1)} %get-tuple-element.37.refs_2_, f32[32,8,128]{2,1,0:T(8,128)S(1)} %all_to_all.43.refs_3_, ...), custom_call_target="tpu_custom_call" | custom-call | tf_op jit(solution)/shard_map/arnoldi_step/pallas_call | solution.py:456
  123.5 10.3 %all_to_all.44.refs_3_ = f32[32,8,128]{2,1,0:T(8,128)S(1)} all-to-all(f32[32,8,128]{2,1,0:T(8,128)S(1)} %get-tuple-element.48), channel_id=1, replica_groups=mesh['wake'=16,'col'=2] {'wake','col'}, dimensions={0} | all-to-all | bytes 262144 | tf_op jit(solution)/shard_map/all_to_all | solution.py:568
  133.8 1.9 %arnoldi_step.11 = (f32[256,128]{1,0:T(8,128)S(1)}, f32[8,128]{1,0:T(8,128)S(1)}, f32[32,8,128]{2,1,0:T(8,128)S(1)}) custom-call(s32[2]{0:T(128)S(1)} %pad_add_fusion.place_ref.refs_0_, s32[16]{0:T(128)S(1)} %bitcast.44, s32[8]{0:T(128)S(1)} %get-tuple-element.37.refs_2_, f32[32,8,128]{2,1,0:T(8,128)S(1)} %all_to_all.44.refs_3_, ...), custom_call_target="tpu_custom_call" | custom-call | tf_op jit(solution)/shard_map/arnoldi_step/pallas_call | solution.py:456
  135.7 10.3 %all_to_all.45.image_ref = f32[32,8,128]{2,1,0:T(8,128)S(1)} all-to-all(f32[32,8,128]{2,1,0:T(8,128)S(1)} %get-tuple-element.50), channel_id=1, replica_groups=mesh['wake'=16,'col'=2] {'wake','col'}, dimensions={0} | all-to-all | bytes 262144 | tf_op jit(solution)/shard_map/all_to_all | solution.py:574
  146.1 1.6 %finish.1 = f32[8,128]{1,0:T(8,128)} custom-call(s32[2]{0:T(128)S(1)} %pad_add_fusion.place_ref.refs_0_, f32[32,8,128]{2,1,0:T(8,128)S(1)} %all_to_all.45.image_ref, f32[256,128]{1,0:T(8,128)S(1)} %get-tuple-element.39.refs_4_.refs_0_, f32[256,128]{1,0:T(8,128)S(1)} %get-tuple-element.43.refs_5_.refs_1_, f32[256,128]{1,0:T(8,128)S(1)} %get-tuple-element.45.refs_6_.refs_2_, ...), custom_call_target="tpu_custom_call" | custom-call | tf_op jit(solution)/shard_map/finish/pallas_call | solution.py:521
Async XLA Ops:
  2.1 68.8 %collective-permute-start.1 = (f32[32,16384]{1,0:T(8,128)}, f32[32,16384]{1,0:T(8,128)}, u32[]{:S(2)}, u32[]{:S(2)}) collective-permute-start(f32[32,16384]{1,0:T(8,128)} %bitcast.11), channel_id=1, source_target_pairs={{0,1},{1,0},{2,3},{3,2},{4,5},{5,4},{6,7},{7,6},{8,9},{9,8},{10,11... | collective-permute-start | bytes 6291464 | tf_op jit(solution)/shard_map/ppermute | solution.py:559
  5.1 17.0 %all-to-all-start = ((f32[16,5,8,128]{3,2,1,0:T(8,128)}), f32[16,5,8,128]{3,2,1,0:T(8,128)S(1)}, u32[]{:S(2)}, u32[]{:S(2)}) async-start(f32[16,5,8,128]{3,2,1,0:T(8,128)} %pack_nodes.1), calls=%async_computation | async-start | bytes 655360 | tf_op jit(solution)/shard_map/all_to_all | solution.py:563
  11.1 1.2 copy-start.1
  12.3 0.9 copy-start.3
  13.3 0.7 copy-start.6
  15.4 49.8 %collective-permute-start = (f32[1288,128]{1,0:T(8,128)}, f32[1288,128]{1,0:T(8,128)}, u32[]{:S(2)}, u32[]{:S(2)}) collective-permute-start(f32[1288,128]{1,0:T(8,128)} %deal.1), channel_id=1, source_target_pairs={{0,1},{1,0},{2,3},{3,2},{4,5},{5,4},{6,7},{7,6},{8,9},{9,8},{10,11... | collective-permute-start | bytes 1978376 | tf_op jit(solution)/shard_map/ppermute | solution.py:558
  22.1 0.7 copy-start.8
  22.9 48.0 %copy-start = (f32[1,32,16384]{2,1,0:T(8,128)S(1)}, f32[1,32,16384]{2,1,0:T(8,128)}, u32[]{:S(2)}) copy-start(f32[1,32,16384]{2,1,0:T(8,128)} %param.21) | copy-start | bytes 6291460
  22.9 48.0 %copy-start.2 = (f32[16,1,1,128,128]{4,3,2,1,0:T(8,128)S(1)}, f32[16,1,1,128,128]{4,3,2,1,0:T(8,128)}, u32[]{:S(2)}) copy-start(f32[16,1,1,128,128]{4,3,2,1,0:T(8,128)} %param.18) | copy-start | bytes 3145732
  22.9 48.0 %copy-start.4 = (f32[1,32,2048]{2,1,0:T(8,128)S(1)}, f32[1,32,2048]{2,1,0:T(8,128)}, u32[]{:S(2)}) copy-start(f32[1,32,2048]{2,1,0:T(8,128)} %param.20) | copy-start | bytes 786436
  22.9 48.1 %copy-start.5 = (f32[1024]{0:T(1024)S(1)}, f32[1024]{0:T(1024)}, u32[]{:S(2)}) copy-start(f32[1024]{0:T(1024)} %param.17) | copy-start | bytes 12292
  22.9 48.1 %copy-start.7 = (s32[16,1,1]{0,2,1:T(1,128)S(1)}, s32[16,1,1]{0,2,1:T(1,128)}, u32[]{:S(2)}) copy-start(s32[16,1,1]{0,2,1:T(1,128)} %param.19) | copy-start | bytes 196
  59.7 11.2 %all-to-all-start.1 = ((f32[32,8,128]{2,1,0:T(8,128)}), f32[32,8,128]{2,1,0:T(8,128)S(1)}, u32[]{:S(2)}, u32[]{:S(2)}) async-start(f32[32,8,128]{2,1,0:T(8,128)} %get-tuple-element.35), calls=%async_computation.1 | async-start | bytes 262144 | tf_op jit(solution)/shard_map/all_to_all | solution.py:568
